TPU v7x, 32 devices: a whole 2x2x4 slice. The times are simulated.
32 devices in a mesh: ctx: 8 (over z, y), head: 4 (over x, core).
Axes of the slice: x: 2, y: 2, z: 4, core: 2. Of those that a mesh axis runs over, the one named last changes fastest.
Arguments:
- queries: bfloat16 [4096, 2048], P('ctx', 'head'), may hold values from -6 to 6
- keys: bfloat16 [4096, 2048], P('ctx', 'head'), may hold values from -6 to 6
- values: bfloat16 [4096, 2048], P('ctx', 'head'), may hold values from -16 to 16
- out_grad: bfloat16 [4096, 2048], P('ctx', 'head'), may hold values from -6 to 6
- norm_gain: float32 [2048], P('head'), may hold values from 0.1 to 1.9
- doc_lengths: int32 [16], replicated, may hold values from 1 to 2048, 4096 in all
- group_level: int32 [4], replicated, may hold values from 0 to 2
Outputs:
- output: bfloat16 [4096, 2048], P('ctx', 'head')
- query_grad: bfloat16 [4096, 2048], P('ctx', 'head')
- key_grad: bfloat16 [4096, 2048], P('ctx', 'head')
- value_grad: bfloat16 [4096, 2048], P('ctx', 'head')
All inputs are finite; a program needn't handle non-finite values.
Results may differ from a plain program's by a relative error of at most 0.013.
Values may be sent and summed in bfloat16 or wider, within the bound.
A program may use at most 64 MiB of HBM per device.

v0:
```python
import jax
import jax.numpy as jnp
from jax import lax
from jax.sharding import PartitionSpec as P

HEAD_FEATURES = 128
DILATION = 32


EPS = 1e-05


def from_partner(value, axis, distance):
    mask = 2**distance
    pairs = [(source, source ^ mask) for source in range(lax.axis_size(axis))]
    return lax.ppermute(value, axis, pairs)


def document_of(places, ends):
    return jnp.sum((places[..., None] >= ends).astype(jnp.int32), axis=-1, dtype=jnp.int32)


def shards(queries, keys, values, out_grad, norm_gain, doc_lengths, group_level):
    tok_rows, width_dev = queries.shape
    heads_dev = width_dev // HEAD_FEATURES
    ctx_place = lax.axis_index("ctx")
    head_place = lax.axis_index("head")
    picked_total = tok_rows * lax.axis_size("ctx") // DILATION
    picked_dev = tok_rows // DILATION
    full_width = width_dev * lax.axis_size("head")
    logit_scale = HEAD_FEATURES ** (-0.5)
    ends = jnp.cumsum(doc_lengths, dtype=jnp.int32)
    places = ctx_place * tok_rows + jnp.arange(tok_rows, dtype=jnp.int32)
    docs = document_of(places, ends)
    head_ids = head_place * heads_dev + jnp.arange(heads_dev, dtype=jnp.int32)
    offsets = head_ids % DILATION
    group_ids = jnp.arange(group_level.shape[0], dtype=jnp.int32)
    level = jnp.sum(jnp.where(group_ids == head_place, group_level, 0), dtype=jnp.int32)
    rate = jnp.left_shift(jnp.int32(1), level)
    picker = jnp.arange(DILATION, dtype=jnp.int32)[:, None] == offsets[None, :]
    pick_half = picker.astype(jnp.bfloat16)
    pick_full = picker.astype(jnp.float32)
    counter = jnp.arange(picked_total, dtype=jnp.int32)
    far_places = counter[None, :] * DILATION + offsets[:, None]
    far_docs = document_of(far_places, ends)
    far_live = counter % rate == 0
    query_rows = queries.reshape(tok_rows, heads_dev, HEAD_FEATURES)
    key_rows = keys.reshape(tok_rows, heads_dev, HEAD_FEATURES)
    value_rows = values.reshape(tok_rows, heads_dev, HEAD_FEATURES)

    def select(rows):
        wide = (
            rows.reshape(picked_dev, DILATION, heads_dev, HEAD_FEATURES)
            * pick_half[None, :, :, None]
        )
        return jnp.sum(wide, axis=1)

    def spread(rows):
        wide = rows[:, None, :, :] * pick_full[None, :, :, None]
        return wide.reshape(tok_rows, heads_dev, HEAD_FEATURES)

    own_keys = select(key_rows)
    own_values = select(value_rows)
    far_keys, far_values = (
        lax.all_gather(own_keys, "ctx", axis=0, tiled=True),
        lax.all_gather(own_values, "ctx", axis=0, tiled=True),
    )

    def weights(remote_keys):
        near_mask = ((places[:, None] >= places[None, :]) & (docs[:, None] == docs[None, :]))[None]
        far_mask = (
            (far_places[:, None, :] <= places[None, :, None])
            & (far_docs[:, None, :] == docs[None, :, None])
            & far_live[None, None, :]
        )
        nearby_logit = (
            jnp.einsum("qhd,khd->hqk", query_rows, key_rows, preferred_element_type=jnp.float32)
            * logit_scale
        )
        far_score = (
            jnp.einsum("qhd,khd->hqk", query_rows, remote_keys, preferred_element_type=jnp.float32)
            * logit_scale
        )
        top = jnp.maximum(
            jnp.max(jnp.where(near_mask, nearby_logit, -jnp.inf), -1),
            jnp.max(jnp.where(far_mask, far_score, -jnp.inf), -1),
        )
        summed = jnp.sum(
            jnp.where(near_mask, jnp.exp(nearby_logit - top[..., None]), 0.0), -1
        ) + jnp.sum(jnp.where(far_mask, jnp.exp(far_score - top[..., None]), 0.0), -1)
        log_total = top + jnp.log(summed)
        nearby_weight = jnp.where(near_mask, jnp.exp(nearby_logit - log_total[..., None]), 0.0)
        far_weight = jnp.where(far_mask, jnp.exp(far_score - log_total[..., None]), 0.0)
        return (nearby_weight, far_weight)

    nearby_weight, far_weight = weights(far_keys)
    nearby_portion = jnp.einsum(
        "hqk,khd->qhd",
        nearby_weight.astype(jnp.bfloat16),
        value_rows,
        preferred_element_type=jnp.float32,
    )
    far_part = jnp.einsum(
        "hqk,khd->qhd",
        far_weight.astype(jnp.bfloat16),
        far_values,
        preferred_element_type=jnp.float32,
    )
    pieces = (nearby_portion + far_part).astype(jnp.bfloat16)
    flat = pieces.reshape(tok_rows, width_dev).astype(jnp.float32)
    scaled = out_grad.astype(jnp.float32) * norm_gain
    part_sum = jnp.sum(flat, 1)
    part_square = jnp.sum(flat * flat, 1)
    sum_rows, square_rows = lax.psum((part_sum, part_square), "head")
    mean = sum_rows / full_width
    rstd = lax.rsqrt(square_rows / full_width - mean * mean + EPS)
    mean, rstd = (mean, rstd)
    normed = (flat - mean[:, None]) * rstd[:, None]
    grad_sum, grad_proj_sum = lax.psum((jnp.sum(scaled, 1), jnp.sum(scaled * normed, 1)), "head")
    output = (normed * norm_gain).astype(jnp.bfloat16)
    att_grad = (
        rstd[:, None]
        * (scaled - grad_sum[:, None] / full_width - normed * grad_proj_sum[:, None] / full_width)
    ).astype(jnp.bfloat16)
    back_keys, back_values = (far_keys, far_values)
    grad_rows = att_grad.reshape(tok_rows, heads_dev, HEAD_FEATURES)
    query_parts, key_parts, value_parts = ([], [], [])
    nearby_weight, far_weight = weights(back_keys)
    delta = jnp.sum(grad_rows.astype(jnp.float32) * pieces.astype(jnp.float32), -1).T
    nearby_product = jnp.einsum(
        "qhd,khd->hqk", grad_rows, value_rows, preferred_element_type=jnp.float32
    )
    far_dot = jnp.einsum("qhd,khd->hqk", grad_rows, back_values, preferred_element_type=jnp.float32)
    nearby_gradient_slope = (nearby_weight * (nearby_product - delta[..., None])).astype(
        jnp.bfloat16
    )
    far_slope = (far_weight * (far_dot - delta[..., None])).astype(jnp.bfloat16)
    nearby_rounded = nearby_weight.astype(jnp.bfloat16)
    far_round = far_weight.astype(jnp.bfloat16)
    query_portion = jnp.einsum(
        "hqk,khd->qhd", nearby_gradient_slope, key_rows, preferred_element_type=jnp.float32
    )
    query_portion = query_portion + jnp.einsum(
        "hqk,khd->qhd", far_slope, back_keys, preferred_element_type=jnp.float32
    )
    query_parts.append(query_portion * logit_scale)
    key_parts.append(
        jnp.einsum(
            "hqk,qhd->khd", nearby_gradient_slope, query_rows, preferred_element_type=jnp.float32
        )
        * logit_scale
    )
    value_parts.append(
        jnp.einsum("hqk,qhd->khd", nearby_rounded, grad_rows, preferred_element_type=jnp.float32)
    )
    far_key_term = jnp.einsum(
        "hqk,qhd->khd", far_slope, query_rows, preferred_element_type=jnp.float32
    )
    far_value_term = jnp.einsum(
        "hqk,qhd->khd", far_round, grad_rows, preferred_element_type=jnp.float32
    )
    terms = jnp.stack([far_key_term, far_value_term], 1)
    current = terms
    for bit_place in reversed(range(lax.axis_size("ctx").bit_length() - 1)):
        half_rows = current.shape[0] // 2
        lower_rows = current[:half_rows]
        upper_rows = current[half_rows:]
        high_side = jnp.bitwise_and(jnp.right_shift(ctx_place, bit_place), 1) == 1
        outgoing = jnp.where(high_side, lower_rows, upper_rows)
        kept = jnp.where(high_side, upper_rows, lower_rows)
        incoming = from_partner(outgoing, "ctx", bit_place)
        current = kept + incoming
    query_grad = query_parts[0].astype(jnp.bfloat16).reshape(tok_rows, width_dev)
    key_grad = (
        (key_parts[0] + spread(current[:, 0]) * logit_scale)
        .astype(jnp.bfloat16)
        .reshape(tok_rows, width_dev)
    )
    value_grad = (
        (value_parts[0] + spread(current[:, 1])).astype(jnp.bfloat16).reshape(tok_rows, width_dev)
    )
    return (output, query_grad, key_grad, value_grad)


def solution(mesh):
    return jax.shard_map(
        shards,
        mesh=mesh,
        in_specs=(
            P("ctx", "head"),
            P("ctx", "head"),
            P("ctx", "head"),
            P("ctx", "head"),
            P("head"),
            P(),
            P(),
        ),
        out_specs=(P("ctx", "head"), P("ctx", "head"), P("ctx", "head"), P("ctx", "head")),
        check_vma=False,
    )
```

profile of v0, /device:TPU:0, one launch (start us, length us, event | category | flops | bytes accessed | tf_op | source)
XLA Modules:
  0.0 151.8 jit_solution(1174561518717615549)
XLA Ops:
  0.7 1.2 reshape_reshape.6
  1.9 1.3 copy.168
  3.2 1.3 fusion.33
  7.5 1.3 reshape_reshape.7
  9.4 32.3 %all_gather.6 = bf16[128,4,128]{2,0,1:T(8,128)(2,1)S(1)} all-gather(bf16[16,4,128]{2,0,1:T(8,128)(2,1)S(1)} %copy.131), channel_id=1, replica_groups=mesh['ctx'=8,'head'=4] {'ctx'}, dimensions={0}, use_global_device_ids=true | all-gather | bytes 147456 | tf_op jit(solution)/shard_map/all_gather | solution.py:65
  41.7 30.5 %all_gather.7 = bf16[128,4,128]{2,0,1:T(8,128)(2,1)S(1)} all-gather(bf16[16,4,128]{2,0,1:T(8,128)(2,1)S(1)} %copy.135), channel_id=1, replica_groups=mesh['ctx'=8,'head'=4] {'ctx'}, dimensions={0}, use_global_device_ids=true | all-gather | bytes 147456 | tf_op jit(solution)/shard_map/all_gather | solution.py:66
  75.1 1.0 convolution_bitcast_fusion.1
  76.3 1.2 fusion.40
  77.8 6.4 %all-reduce.1 = (f32[512]{0:T(512)}, f32[512]{0:T(512)}) all-reduce(f32[512]{0:T(512)} %get-tuple-element.25, f32[512]{0:T(512)} %get-tuple-element.24), channel_id=1, replica_groups=mesh['ctx'=8,'head'=4] {'head'}, use_global_device_ids=true, to_apply=%region_13.14 | all-reduce | flops 1024 | bytes 8192 | tf_op jit(solution)/shard_map/psum | solution.py:114
  85.5 2.1 %fusion.15 = (f32[512]{0:T(512)}, f32[512]{0:T(512)}) fusion(bf16[512,512]{1,0:T(8,128)(2,1)} %param.10, f32[512]{0:T(512)} %param.11, f32[512]{0:T(512)S(1)} %get-tuple-element.39, f32[512,512]{1,0:T(8,128)S(1)} %copy.137, f32[512]{0:T(512)S(1)} %get-tuple-element.38), kind=kLoop, calls=%fused_computation.33 | loop fusion | flops 1833984 | bytes 1583104 | tf_op jit(solution)/shard_map/reduce_sum | solution.py:119
  87.6 7.5 %all-reduce = (f32[512]{0:T(512)}, f32[512]{0:T(512)}) all-reduce(f32[512]{0:T(512)} %get-tuple-element.27, f32[512]{0:T(512)} %get-tuple-element.26), channel_id=1, replica_groups=mesh['ctx'=8,'head'=4] {'head'}, use_global_device_ids=true, to_apply=%region_17.18 | all-reduce | flops 1024 | bytes 8192 | tf_op jit(solution)/shard_map/psum | solution.py:119
  95.7 2.4 %multiply_convert_fusion.1 = (bf16[512,512]{1,0:T(8,128)(2,1)}, bf16[512,512]{1,0:T(8,128)(2,1)}) fusion(bf16[512,512]{1,0:T(8,128)(2,1)} %param.10, f32[512,512]{1,0:T(8,128)S(1)} %copy.137, f32[512]{0:T(512)} %get-tuple-element.30, f32[512]{0:T(512)S(1)} %broadcast_multiply_fusion, f32[512]{0:T(512)} %param.11, f32[512]{0:T(512)} %copy-done.20, ...), kind=kLoop, calls=%fused_computation.30 | loop fusion | flops 3145728 | bytes 2631680 | tf_op jit(solution)/shard_map/convert_element_type | solution.py:124
  98.2 2.1 %copy.138 = bf16[512,512]{0,1:T(8,128)(2,1)} copy(bf16[512,512]{1,0:T(8,128)(2,1)} %get-tuple-element.34) | data formatting | bytes 1048576 | tf_op jit(solution)/shard_map/convert_element_type | solution.py:124
  100.3 1.3 multiply_reduce_fusion
  101.6 1.9 %convolution_bitcast_fusion.5 = f32[128,1,4,128]{3,0,2,1:T(8,128)S(1)} fusion(bf16[512,4,128]{0,2,1:T(8,128)(2,1)} %bitcast.116, f32[4,512,128]{1,2,0:T(8,128)} %copy-done.2, f32[4,512]{1,0:T(4,128)S(1)} %log_add_fusion, s32[512]{0:T(512)S(1)} %convert_reduce_fusion.1, s32[4,128]{1,0:T(4,128)} %copy-done.17, s32[512]{0:T(512)S(1)} %iota_add_fusion, ...), kind=kOutput, calls=%fused_computation.27 | convolution fusion | flops 68943872 | bytes 1851520 | tf_op jit(solution)/shard_map/hqk,qhd->khd/dot_general | solution.py:159
  103.5 1.3 fusion.11
  106.6 3.9 %multiply_convert_fusion = bf16[4,512,512]{1,2,0:T(8,128)(2,1)S(1)} fusion(f32[4,512,512]{1,2,0:T(8,128)} %copy-done.1, bf16[512,4,128]{0,2,1:T(8,128)(2,1)} %bitcast.117, f32[4,512]{1,0:T(4,128)} %bitcast.124, f32[4,512]{1,0:T(4,128)S(1)} %log_add_fusion, pred[512,512]{0,1:T(8,128)(4,1)S(1)} %compare_and_fusion, bf16[512,512]{1,0:T(8,128)(2,1)} %param.9), kind=kOutput, calls=%fused_computation | convolution fusion | flops 274726912 | bytes 7618560 | tf_op jit(solution)/shard_map/qhd,khd->hqk/dot_general | solution.py:130
  110.6 8.3 %collective-permute-done = f32[64,2,4,128]{3,0,2,1:T(8,128)} collective-permute-done((f32[64,2,4,128]{3,0,2,1:T(8,128)}, f32[64,2,4,128]{3,0,2,1:T(8,128)}, u32[]{:S(2)}, u32[]{:S(2)}) %collective-permute-start) | collective-permute-done | bytes 262176 | tf_op jit(solution)/shard_map/ppermute | solution.py:16
  118.8 1.0 select_add_fusion
  120.5 1.4 convolution_bitcast_fusion
  122.0 4.3 %collective-permute-done.1 = f32[32,2,4,128]{3,0,2,1:T(8,128)} collective-permute-done((f32[32,2,4,128]{3,0,2,1:T(8,128)}, f32[32,2,4,128]{3,0,2,1:T(8,128)}, u32[]{:S(2)}, u32[]{:S(2)}) %collective-permute-start.1) | collective-permute-done | bytes 131104 | tf_op jit(solution)/shard_map/ppermute | solution.py:16
  127.2 2.9 %collective-permute-start.2 = (f32[16,2,4,128]{3,0,2,1:T(8,128)S(1)}, f32[16,2,4,128]{3,0,2,1:T(8,128)S(1)}, u32[]{:S(2)}, u32[]{:S(2)}) collective-permute-start(f32[16,2,4,128]{3,0,2,1:T(8,128)S(1)} %slice_select_fusion.1), channel_id=1, source_target_pairs={{0,4},{4,0},{8,12},{12,8},{16,20},{20,16},{24,28},{28,24},{1,5},{5... | collective-permute-start | bytes 196616 | tf_op jit(solution)/shard_map/ppermute | solution.py:16
  130.2 2.5 %fusion.10 = bf16[512,4,128]{0,2,1:T(8,128)(2,1)} fusion(f32[512,4,128]{0,2,1:T(8,128)} %convolution_bitcast_fusion, bf16[128,4,128]{2,0,1:T(8,128)(2,1)S(1)} %all_gather.6, bf16[4,512,128]{1,2,0:T(8,128)(2,1)} %copy-done.9), kind=kOutput, calls=%fused_computation.22 | convolution fusion | flops 67895296 | bytes 2228224 | tf_op jit(solution)/shard_map/hqk,khd->qhd/dot_general | solution.py:143
  132.8 2.0 %copy.154 = bf16[512,512]{1,0:T(8,128)(2,1)} copy(bf16[512,512]{0,1:T(8,128)(2,1)} %bitcast.120) | data formatting | bytes 1048576
  134.9 1.1 mul.183
  136.0 2.5 %copy.153 = f32[512,4,128]{0,2,1:T(8,128)} copy(f32[512,4,128]{2,0,1:T(8,128)} %bitcast.114) | data formatting | bytes 2097152 | tf_op jit(solution)/shard_map/mul | solution.py:59
  138.5 4.6 %fusion.12 = bf16[512,4,128]{0,2,1:T(8,128)(2,1)} fusion(bf16[512,4,128]{0,2,1:T(8,128)(2,1)} %bitcast.118, f32[512,4,128]{0,2,1:T(8,128)} %copy.153, f32[512,4]{0,1:T(4,128)S(1)} %mul.178, f32[4,512,512]{1,2,0:T(8,128)} %copy-done.1, f32[4,512]{1,0:T(4,128)S(1)} %log_add_fusion, pred[512,512]{0,1:T(8,128)(4,1)S(1)} %copy-done.7), kind=kOutput, calls=%fused_computation.24 | convolution fusion | flops 273416192 | bytes 6569984 | tf_op jit(solution)/shard_map/hqk,qhd->khd/dot_general | solution.py:154
  143.1 2.0 %copy.156 = bf16[512,512]{1,0:T(8,128)(2,1)} copy(bf16[512,512]{0,1:T(8,128)(2,1)} %bitcast.122) | data formatting | bytes 1048576
  145.1 1.1 mul.175
  146.2 2.6 %copy.151 = f32[512,4,128]{0,2,1:T(8,128)} copy(f32[512,4,128]{2,0,1:T(8,128)} %bitcast.115) | data formatting | bytes 2097152 | tf_op jit(solution)/shard_map/mul | solution.py:59
  148.8 2.1 %fusion.9 = bf16[512,4,128]{0,2,1:T(8,128)(2,1)S(1)} fusion(bf16[4,512,512]{1,2,0:T(8,128)(2,1)S(1)} %multiply_convert_fusion, f32[512,4,128]{0,2,1:T(8,128)} %copy.151, f32[512,4]{0,1:T(4,128)S(1)} %mul.178, bf16[512,512]{1,0:T(8,128)(2,1)S(1)} %copy-done), kind=kOutput, calls=%fused_computation.21 | convolution fusion | flops 269746176 | bytes 4202496 | tf_op jit(solution)/shard_map/hqk,qhd->khd/dot_general | solution.py:148
  150.8 1.0 copy.155
  (87 shorter events, 11.6 us)
Async XLA Ops:
  0.6 71.6 %copy-start = (bf16[512,512]{1,0:T(8,128)(2,1)S(1)}, bf16[512,512]{1,0:T(8,128)(2,1)}, u32[]{:S(2)}) copy-start(bf16[512,512]{1,0:T(8,128)(2,1)} %param.7) | copy-start | bytes 1572868
  5.2 68.4 %copy-start.23 = (pred[128]{0:T(512)(128)(4,1)}, pred[128]{0:T(512)(128)(4,1)S(1)}, u32[]{:S(2)}) copy-start(pred[128]{0:T(512)(128)(4,1)S(1)} %fusion.35) | copy-start | bytes 388
  6.0 67.7 %copy-start.15 = (s32[4,128]{1,0:T(4,128)}, s32[4,128]{1,0:T(4,128)S(1)}, u32[]{:S(2)}) copy-start(s32[4,128]{1,0:T(4,128)S(1)} %broadcast_add_fusion) | copy-start | bytes 6148
  7.2 66.5 %copy-start.17 = (s32[4,128]{1,0:T(4,128)}, s32[4,128]{1,0:T(4,128)S(1)}, u32[]{:S(2)}) copy-start(s32[4,128]{1,0:T(4,128)S(1)} %convert_reduce_fusion) | copy-start | bytes 6148
  7.4 99.2 %copy-start.6 = (pred[512,512]{0,1:T(8,128)(4,1)}, pred[512,512]{0,1:T(8,128)(4,1)S(1)}, u32[]{:S(2)}) copy-start(pred[512,512]{0,1:T(8,128)(4,1)S(1)} %compare_and_fusion) | copy-start | bytes 786436
  72.2 4.0 %copy-start.12 = (bf16[128,4,128]{2,0,1:T(8,128)(2,1)}, bf16[128,4,128]{2,0,1:T(8,128)(2,1)S(1)}, u32[]{:S(2)}) copy-start(bf16[128,4,128]{2,0,1:T(8,128)(2,1)S(1)} %all_gather.7) | copy-start | bytes 393220
  73.1 3.1 %copy-start.1 = (f32[4,512,512]{1,2,0:T(8,128)}, f32[4,512,512]{1,2,0:T(8,128)S(1)}, u32[]{:S(2)}) copy-start(f32[4,512,512]{1,2,0:T(8,128)S(1)} %get-tuple-element.43) | copy-start | bytes 12582916
  73.1 2.0 %copy-start.14 = (bf16[512,512]{1,0:T(8,128)(2,1)S(1)}, bf16[512,512]{1,0:T(8,128)(2,1)}, u32[]{:S(2)}) copy-start(bf16[512,512]{1,0:T(8,128)(2,1)} %param.9) | copy-start | bytes 1572868
  73.6 2.6 %copy-start.2 = (f32[4,512,128]{1,2,0:T(8,128)}, f32[4,512,128]{1,2,0:T(8,128)S(1)}, u32[]{:S(2)}) copy-start(f32[4,512,128]{1,2,0:T(8,128)S(1)} %get-tuple-element.45) | copy-start | bytes 3145732
  75.1 1.1 copy-start.16
  75.1 1.1 copy-start.18
  75.1 1.1 copy-start.24
  84.9 0.6 copy-start.19
  84.9 2.6 %copy-start.20 = (f32[512]{0:T(512)}, f32[512]{0:T(512)S(1)}, u32[]{:S(2)}) copy-start(f32[512]{0:T(512)S(1)} %get-tuple-element.39) | copy-start | bytes 6148
  98.2 5.3 %copy-start.3 = (f32[4,512,128]{1,2,0:T(8,128)S(1)}, f32[4,512,128]{1,2,0:T(8,128)}, u32[]{:S(2)}) copy-start(f32[4,512,128]{1,2,0:T(8,128)} %copy-done.2) | copy-start | bytes 3145732
  100.3 3.2 %copy-start.8 = (bf16[512,512]{0,1:T(8,128)(2,1)S(1)}, bf16[512,512]{0,1:T(8,128)(2,1)}, u32[]{:S(2)}) copy-start(bf16[512,512]{0,1:T(8,128)(2,1)} %copy.138) | copy-start | bytes 1572868
  100.3 3.2 %copy-start.13 = (bf16[128,4,128]{2,0,1:T(8,128)(2,1)S(1)}, bf16[128,4,128]{2,0,1:T(8,128)(2,1)}, u32[]{:S(2)}) copy-start(bf16[128,4,128]{2,0,1:T(8,128)(2,1)} %copy-done.12) | copy-start | bytes 393220
  101.6 5.0 %copy-start.21 = (f32[512,4]{0,1:T(4,128)}, f32[512,4]{0,1:T(4,128)S(1)}, u32[]{:S(2)}) copy-start(f32[512,4]{0,1:T(4,128)S(1)} %multiply_reduce_fusion) | copy-start | bytes 24580
  103.5 3.1 %copy-start.10 = (f32[128,1,4,128]{3,0,2,1:T(8,128)}, f32[128,1,4,128]{3,0,2,1:T(8,128)S(1)}, u32[]{:S(2)}) copy-start(f32[128,1,4,128]{3,0,2,1:T(8,128)S(1)} %convolution_bitcast_fusion.5) | copy-start | bytes 786436
  104.8 1.8 %copy-start.9 = (bf16[4,512,128]{1,2,0:T(8,128)(2,1)}, bf16[4,512,128]{1,2,0:T(8,128)(2,1)S(1)}, u32[]{:S(2)}) copy-start(bf16[4,512,128]{1,2,0:T(8,128)(2,1)S(1)} %fusion.11) | copy-start | bytes 1572868
  105.1 0.7 copy-start.4
  106.6 12.3 %collective-permute-start = (f32[64,2,4,128]{3,0,2,1:T(8,128)}, f32[64,2,4,128]{3,0,2,1:T(8,128)}, u32[]{:S(2)}, u32[]{:S(2)}) collective-permute-start(f32[64,2,4,128]{3,0,2,1:T(8,128)} %broadcast_select_fusion), channel_id=1, source_target_pairs={{0,16},{4,20},{8,24},{12,28},{16,0},{20,4},{24,8},{28,12},{1,17},{... | collective-permute-start | bytes 786440 | tf_op jit(solution)/shard_map/ppermute | solution.py:16
  106.6 12.2 %copy-start.5 = (f32[128,1,4,128]{3,0,2,1:T(8,128)S(1)}, f32[128,1,4,128]{3,0,2,1:T(8,128)}, u32[]{:S(2)}) copy-start(f32[128,1,4,128]{3,0,2,1:T(8,128)} %copy-done.4) | copy-start | bytes 786436
  106.6 12.2 %copy-start.11 = (f32[128,1,4,128]{3,0,2,1:T(8,128)S(1)}, f32[128,1,4,128]{3,0,2,1:T(8,128)}, u32[]{:S(2)}) copy-start(f32[128,1,4,128]{3,0,2,1:T(8,128)} %copy-done.10) | copy-start | bytes 786436
  110.6 22.1 %copy-start.22 = (f32[32,4]{0,1:T(4,128)S(1)}, f32[32,4]{0,1:T(4,128)}, u32[]{:S(2)}) copy-start(f32[32,4]{0,1:T(4,128)} %get-tuple-element.40) | copy-start | bytes 1540
  120.5 5.7 %collective-permute-start.1 = (f32[32,2,4,128]{3,0,2,1:T(8,128)}, f32[32,2,4,128]{3,0,2,1:T(8,128)}, u32[]{:S(2)}, u32[]{:S(2)}) collective-permute-start(f32[32,2,4,128]{3,0,2,1:T(8,128)} %slice_select_fusion), channel_id=1, source_target_pairs={{0,8},{4,12},{8,0},{12,4},{16,24},{20,28},{24,16},{28,20},{1,9},{5... | collective-permute-start | bytes 393224 | tf_op jit(solution)/shard_map/ppermute | solution.py:16
  122.0 16.6 %copy-start.7 = (pred[512,512]{0,1:T(8,128)(4,1)S(1)}, pred[512,512]{0,1:T(8,128)(4,1)}, u32[]{:S(2)}) copy-start(pred[512,512]{0,1:T(8,128)(4,1)} %copy-done.6) | copy-start | bytes 786436
  127.2 7.6 %collective-permute-start.2 = (f32[16,2,4,128]{3,0,2,1:T(8,128)S(1)}, f32[16,2,4,128]{3,0,2,1:T(8,128)S(1)}, u32[]{:S(2)}, u32[]{:S(2)}) collective-permute-start(f32[16,2,4,128]{3,0,2,1:T(8,128)S(1)} %slice_select_fusion.1), channel_id=1, source_target_pairs={{0,4},{4,0},{8,12},{12,8},{16,20},{20,16},{24,28},{28,24},{1,5},{5... | collective-permute-start | bytes 196616 | tf_op jit(solution)/shard_map/ppermute | solution.py:16
where the time goes:
time: 153 us; the launch traced here: 152 us
  blocking collectives  76.7 us (50%)
  matrix products  21.7 us (14%)
  local copies, waits for them, and re-layouts  20.9 us (14%)
  other arithmetic  15.3 us (10%)
  waiting for transfers between devices  12.6 us (8%)
  starting transfers between devices  2.95 us (2%)
  between operations  1.75 us (1%)
    all_gather x1, blocking collectives, shards(): lax.all_gather(own_keys, 'ctx', axis=0, tiled=True)  32.3 us
    all_gather x1, blocking collectives, shards(): lax.all_gather(own_values, 'ctx', axis=0, tiled=True)  30.5 us
    ppermute x3, waiting for transfers between devices, from_partner(): return lax.ppermute(value, axis, pairs)  12.6 us
    psum x1, blocking collectives, shards(): lax.psum((jnp.sum(scaled, 1), jnp.sum(scaled * normed, 1)), 'head')  7.48 us
    mul x7, local copies, waits for them, and re-layouts, spread(): wide = rows[:, None, :, :] * pick_full[None, :, :, None]  7.37 us
    unnamed x53, local copies, waits for them, and re-layouts  6.48 us
    psum x1, blocking collectives, shards(): sum_rows, square_rows = lax.psum((part_sum, part_square), 'head')  6.38 us
    dot_general x1, matrix products, shards(): jnp.einsum('hqk,qhd->khd', nearby_rounded, grad_rows, preferred_element_t...  4.56 us
  transfers between devices with their start and end apart: 3, of which 2 were waited for; matrix products, arithmetic and copies ran while one was open for 7% of the time, Pallas kernels for 0%

commit v1 on v0

v1 whole, which is shorter than its diff:
```python
import functools
import math

import jax
import jax.numpy as jnp
from jax import lax
from jax.experimental import pallas as pl
from jax.experimental.pallas import tpu as pltpu
from jax.sharding import PartitionSpec as P

HEAD_FEATURES = 128
DILATION = 32
EPS = 1e-05
HIDDEN = -1e30
MESH = pl.DeviceIdType.MESH
F32 = jnp.float32
BF16 = jnp.bfloat16


def dot(a, b, left=1, right=0):
    return lax.dot_general(a, b, (((left,), (right,)), ((), ())), preferred_element_type=F32)


def iota(shape, dim):
    return lax.broadcasted_iota(jnp.int32, shape, dim)


def kernel(
    ctx_size, head_size, reach, group_heads,
    q_ref, k_ref, v_ref, og_ref, gain_ref, len_ref, level_ref,
    out_ref, dq_ref, dk_ref, dv_ref,
    far_ref, term_ref, back_ref, stat_ref, stats_ref,
    bias_ref, p_ref, pf_ref, ds_ref, sc_ref, o_ref, dqf_ref, own_ref, dkn_ref, dvn_ref,
    far_send, far_recv, back_send, back_recv, stat_send, stat_recv,
):
    toks, width = q_ref.shape
    heads = width // HEAD_FEATURES
    picked = toks // DILATION
    slots = reach + 1
    far_rows = slots * picked
    half = toks // 2
    full = width * head_size
    scale = HEAD_FEATURES ** (-0.5)
    scale2 = scale * math.log2(math.e)
    c = lax.axis_index("ctx")
    hp = lax.axis_index("head")

    def cols(h):
        return slice(h * HEAD_FEATURES, (h + 1) * HEAD_FEATURES)

    def wide_cols(h):
        return slice(width + h * HEAD_FEATURES, width + (h + 1) * HEAD_FEATURES)

    blocks = [(b * half, (b + 1) * half) for b in range(2)]

    for d in range(1, slots):
        @pl.when(c < d)
        def _():
            far_ref[d] = jnp.zeros(far_ref.shape[1:], BF16)

        @pl.when(c + d >= ctx_size)
        def _():
            back_ref[d - 1] = jnp.zeros(back_ref.shape[1:], BF16)

    barrier = pltpu.get_barrier_semaphore()
    for d in range(1, slots):
        @pl.when(c + d < ctx_size)
        def _():
            pl.semaphore_signal(barrier, inc=1, device_id=(c + d, hp), device_id_type=MESH)

        @pl.when(c >= d)
        def _():
            pl.semaphore_signal(barrier, inc=1, device_id=(c - d, hp), device_id_type=MESH)
    for e in range(1, head_size):
        peer = lax.rem(hp + e, head_size)
        pl.semaphore_signal(barrier, inc=1, device_id=(c, peer), device_id_type=MESH)

    def offset_of(h):
        return lax.rem(hp * heads + h, DILATION)

    row_of = iota((picked, toks), 0) * DILATION
    place_in = iota((picked, toks), 1)
    for h in range(heads):
        pick = jnp.where(place_in == row_of + offset_of(h), 1.0, 0.0).astype(BF16)
        far_ref[0, :, cols(h)] = dot(pick, k_ref[:, cols(h)]).astype(BF16)
        far_ref[0, :, wide_cols(h)] = dot(pick, v_ref[:, cols(h)]).astype(BF16)

    before = jnp.minimum(c, reach)
    after = jnp.minimum(ctx_size - 1 - c, reach)
    pl.semaphore_wait(barrier, before + after + (head_size - 1))

    def far_copy(d):
        return pltpu.make_async_remote_copy(
            src_ref=far_ref.at[0], dst_ref=far_ref.at[d],
            send_sem=far_send.at[d - 1], recv_sem=far_recv.at[d - 1],
            device_id=(c + d, hp), device_id_type=MESH,
        )

    def back_copy(d):
        return pltpu.make_async_remote_copy(
            src_ref=term_ref.at[d - 1], dst_ref=back_ref.at[d - 1],
            send_sem=back_send.at[d - 1], recv_sem=back_recv.at[d - 1],
            device_id=(c - d, hp), device_id_type=MESH,
        )

    def stat_copy(e):
        return pltpu.make_async_remote_copy(
            src_ref=stat_ref, dst_ref=stats_ref.at[e - 1],
            send_sem=stat_send.at[e - 1], recv_sem=stat_recv.at[e - 1],
            device_id=(c, lax.rem(hp + e, head_size)), device_id_type=MESH,
        )

    for d in range(1, slots):
        @pl.when(c + d < ctx_size)
        def _():
            far_copy(d).start()

    place_q = iota((1, toks), 1) + c * toks
    first = jnp.zeros((1, toks), jnp.int32)
    end = jnp.int32(0)
    for i in range(len_ref.shape[0]):
        end = end + len_ref[i]
        first = jnp.maximum(first, jnp.where(place_q >= end, end, 0))
    for low, high in blocks:
        place_k = iota((high, half), 0) + c * toks
        seen = (place_k <= place_q[:, low:high]) & (place_k >= first[:, low:high])
        bias_ref[0:high, low:high] = jnp.where(seen, 0.0, HIDDEN)

    tops, sums = [], []
    for h in range(heads):
        values_t = v_ref[:, cols(h)].T
        top_parts, sum_parts = [], []
        for low, high in blocks:
            logit = dot(k_ref[0:high, cols(h)], q_ref[low:high, cols(h)], 1, 1)
            logit = logit * scale2 + bias_ref[0:high, low:high]
            top = jnp.max(logit, axis=0, keepdims=True)
            weight = jnp.exp2(logit - top)
            top_parts.append(top)
            sum_parts.append(jnp.sum(weight, axis=0, keepdims=True))
            weight = weight.astype(BF16)
            p_ref[h, 0:high, low:high] = weight
            o_ref[h, :, low:high] = dot(values_t[:, 0:high], weight)
        tops.append(jnp.concatenate(top_parts, axis=1))
        sums.append(jnp.concatenate(sum_parts, axis=1))
        scaled = og_ref[:, cols(h)].astype(F32) * gain_ref[:, cols(h)]
        sc_ref[h] = scaled.T

    for d in range(1, slots):
        @pl.when(c >= d)
        def _():
            far_copy(d).wait_recv()

    row = iota((far_rows, toks), 0)
    counter = (c - row // picked) * picked + row % picked
    near_scale, far_scale = [], []
    stats = [jnp.zeros((1, toks), F32) for _ in range(4)]
    for h in range(heads):
        far_k = far_ref[:, :, cols(h)].reshape(far_rows, HEAD_FEATURES)
        far_v = far_ref[:, :, wide_cols(h)].reshape(far_rows, HEAD_FEATURES)
        level = level_ref[(hp * heads + h) // group_heads]
        skip = jnp.left_shift(jnp.int32(1), level) - 1
        place_k = counter * DILATION + offset_of(h)
        seen = (place_k <= place_q) & (place_k >= first) & ((counter & skip) == 0)
        logit = jnp.where(seen, dot(far_k, q_ref[:, cols(h)], 1, 1) * scale2, HIDDEN)
        top = jnp.maximum(tops[h], jnp.max(logit, axis=0, keepdims=True))
        weight = jnp.exp2(logit - top)
        shrink = jnp.exp2(tops[h] - top)
        inverse = 1.0 / (sums[h] * shrink + jnp.sum(weight, axis=0, keepdims=True))
        weight = weight.astype(BF16)
        pf_ref[h] = weight
        near_scale.append(shrink * inverse)
        far_scale.append(inverse)
        attended = (o_ref[h] * near_scale[h] + dot(far_v, weight, 0, 0) * inverse).astype(BF16)
        attended = attended.astype(F32)
        o_ref[h] = attended
        scaled = sc_ref[h]
        terms = (attended, attended * attended, scaled, scaled * attended)
        stats = [s + jnp.sum(t, axis=0, keepdims=True) for s, t in zip(stats, terms)]

    for i in range(4):
        stat_ref[i : i + 1, :] = stats[i]
    stat_ref[4:8, :] = jnp.zeros((4, toks), F32)
    for e in range(1, head_size):
        stat_copy(e).start()
    for e in range(1, head_size):
        stat_copy(e).wait_recv()
    total = stat_ref[...]
    for e in range(1, head_size):
        total = total + stats_ref[e - 1]
    total = total / full
    mean, square, grad_mean, cross = (total[i : i + 1, :] for i in range(4))
    rstd = lax.rsqrt(square - mean * mean + EPS)
    shift = -mean * rstd
    proj = rstd * (cross - mean * grad_mean)

    for h in range(heads):
        attended = o_ref[h]
        normed = attended * rstd + shift
        out_ref[:, cols(h)] = (normed.T * gain_ref[:, cols(h)]).astype(BF16)
        grad = rstd * (sc_ref[h] - grad_mean - normed * proj)
        sc_ref[h] = grad
        grad = (grad * far_scale[h]).astype(BF16)
        delta = jnp.sum(grad.astype(F32) * attended, axis=0, keepdims=True)
        far_k = far_ref[:, :, cols(h)].reshape(far_rows, HEAD_FEATURES)
        far_v = far_ref[:, :, wide_cols(h)].reshape(far_rows, HEAD_FEATURES)
        weight = pf_ref[h]
        slope = (weight.astype(F32) * (dot(far_v, grad) - delta)).astype(BF16)
        dqf_ref[h] = dot(far_k, slope, 0, 0)
        key_term = dot(slope, q_ref[:, cols(h)]) * scale
        value_term = dot(weight, grad, 1, 1)
        own_ref[:, cols(h)] = key_term[0:picked]
        own_ref[:, wide_cols(h)] = value_term[0:picked]
        term_ref[:, :, cols(h)] = (
            key_term[picked:].astype(BF16).reshape(reach, picked, HEAD_FEATURES)
        )
        term_ref[:, :, wide_cols(h)] = (
            value_term[picked:].astype(BF16).reshape(reach, picked, HEAD_FEATURES)
        )

    for d in range(1, slots):
        @pl.when(c >= d)
        def _():
            back_copy(d).start()

    for h in range(heads):
        grad = (sc_ref[h] * near_scale[h]).astype(BF16)
        delta = jnp.sum(grad.astype(F32) * o_ref[h], axis=0, keepdims=True)
        keys_t = k_ref[:, cols(h)].T
        for low, high in blocks:
            product = dot(v_ref[0:high, cols(h)], grad[:, low:high])
            weight = p_ref[h, 0:high, low:high].astype(F32)
            slope = (weight * (product - delta[:, low:high])).astype(BF16)
            ds_ref[0:high, low:high] = slope
            query_grad = dot(keys_t[:, 0:high], slope) + dqf_ref[h, :, low:high]
            dq_ref[low:high, cols(h)] = (query_grad * scale).T.astype(BF16)
        for low, high in blocks:
            dkn_ref[low:high, cols(h)] = (
                dot(ds_ref[low:high, low:toks], q_ref[low:toks, cols(h)]) * scale
            )
            dvn_ref[low:high, cols(h)] = dot(p_ref[h, low:high, low:toks], grad[:, low:toks], 1, 1)

    for d in range(1, slots):
        @pl.when(c + d < ctx_size)
        def _():
            back_copy(d).wait_recv()
    mine = own_ref[...]
    for d in range(1, slots):
        mine = mine + back_ref[d - 1].astype(F32)
    upper = mine.astype(BF16)
    lower = (mine - upper.astype(F32)).astype(BF16)
    both = jnp.concatenate([upper, lower], axis=0)
    spot = iota((toks, 2 * picked), 0)
    target = iota((toks, 2 * picked), 1) % picked * DILATION
    for h in range(heads):
        place = jnp.where(spot == target + offset_of(h), 1.0, 0.0).astype(BF16)
        dk_ref[:, cols(h)] = (dkn_ref[:, cols(h)] + dot(place, both[:, cols(h)])).astype(BF16)
        dv_ref[:, cols(h)] = (dvn_ref[:, cols(h)] + dot(place, both[:, wide_cols(h)])).astype(BF16)

    for d in range(1, slots):
        @pl.when(c + d < ctx_size)
        def _():
            far_copy(d).wait_send()

        @pl.when(c >= d)
        def _():
            back_copy(d).wait_send()
    for e in range(1, head_size):
        stat_copy(e).wait_send()


def shards(queries, keys, values, out_grad, norm_gain, doc_lengths, group_level):
    toks, width = queries.shape
    heads = width // HEAD_FEATURES
    ctx_size, head_size = lax.axis_size("ctx"), lax.axis_size("head")
    group_heads = heads * head_size // group_level.shape[0]
    picked = toks // DILATION
    reach = max(ctx_size // 2, 1)
    slots = reach + 1
    vmem = pl.BlockSpec(memory_space=pltpu.VMEM)
    smem = pl.BlockSpec(memory_space=pltpu.SMEM)
    grads = jax.ShapeDtypeStruct((toks, width), BF16)
    return pl.pallas_call(
        functools.partial(kernel, ctx_size, head_size, reach, group_heads),
        out_shape=(grads,) * 4,
        in_specs=[vmem] * 5 + [smem] * 2,
        out_specs=(vmem,) * 4,
        scratch_shapes=[
            pltpu.VMEM((slots, picked, 2 * width), BF16),
            pltpu.VMEM((reach, picked, 2 * width), BF16),
            pltpu.VMEM((reach, picked, 2 * width), BF16),
            pltpu.VMEM((8, toks), F32),
            pltpu.VMEM((head_size - 1, 8, toks), F32),
            pltpu.VMEM((toks, toks), F32),
            pltpu.VMEM((heads, toks, toks), BF16),
            pltpu.VMEM((heads, slots * picked, toks), BF16),
            pltpu.VMEM((toks, toks), BF16),
            pltpu.VMEM((heads, HEAD_FEATURES, toks), F32),
            pltpu.VMEM((heads, HEAD_FEATURES, toks), F32),
            pltpu.VMEM((heads, HEAD_FEATURES, toks), F32),
            pltpu.VMEM((picked, 2 * width), F32),
            pltpu.VMEM((toks, width), F32),
            pltpu.VMEM((toks, width), F32),
            pltpu.SemaphoreType.DMA((reach,)),
            pltpu.SemaphoreType.DMA((reach,)),
            pltpu.SemaphoreType.DMA((reach,)),
            pltpu.SemaphoreType.DMA((reach,)),
            pltpu.SemaphoreType.DMA((head_size - 1,)),
            pltpu.SemaphoreType.DMA((head_size - 1,)),
        ],
        compiler_params=pltpu.CompilerParams(
            collective_id=0, has_side_effects=True, vmem_limit_bytes=48 * 1024 * 1024
        ),
    )(queries, keys, values, out_grad, norm_gain.reshape(1, width), doc_lengths, group_level)


def solution(mesh):
    split = P("ctx", "head")
    return jax.shard_map(
        shards,
        mesh=mesh,
        in_specs=(split, split, split, split, P("head"), P(), P()),
        out_specs=(split, split, split, split),
        check_vma=False,
    )
```

time: 153 us -> 31.6 us (0.21)
  blocking collectives: 76.7 us -> 0 us
  Pallas kernels: 0 us -> 21.9 us
  matrix products: 21.7 us -> 0 us
  other arithmetic: 15.3 us -> 0 us
  waiting for transfers between devices: 12.6 us -> 0 us
  local copies, waits for them, and re-layouts: 20.9 us -> 8.67 us
  starting transfers between devices: 2.95 us -> 0 us
    all_gather x2 -> x0, blocking collectives: 62.8 us -> none  [the longest x1 32.3 us: shards(): lax.all_gather(own_keys, 'ctx', axis=0, tiled=True)]
    pallas_call x0 -> x1, Pallas kernels: none -> 21.9 us  [shards(): pl.pallas_call(functools.partial(kernel, ctx_size, head_size, reach, grou...]
    dot_general x12 -> x0, matrix products: 21.7 us -> none  [the longest x1 4.56 us: shards(): jnp.einsum('hqk,qhd->khd', nearby_rounded, grad_rows, preferred_element_t...]
    psum x2 -> x0, blocking collectives: 13.9 us -> none  [the longest x1 7.48 us: shards(): lax.psum((jnp.sum(scaled, 1), jnp.sum(scaled * normed, 1)), 'head')]
    ppermute x3 -> x0, waiting for transfers between devices: 12.6 us -> none  [from_partner(): return lax.ppermute(value, axis, pairs)]
    mul x7 -> x0, local copies, waits for them, and re-layouts: 7.37 us -> none  [spread(): wide = rows[:, None, :, :] * pick_full[None, :, :, None]]
    reduce_sum x8 -> x0, other arithmetic: 6.82 us -> none  [the longest x1 2.06 us: shards(): jnp.sum(scaled, 1)]
    another operation x3 -> x0, local copies, waits for them, and re-layouts: 3.21 us -> none  [the longest x2 2.48 us: select(): rows.reshape(picked_dev, DILATION, heads_dev, HEAD_FEATURES)]
  transfers between devices with their start and end apart: 3 -> 0, of which waited for: 2 -> 0; matrix products, arithmetic and copies ran while one was open for 7% -> 0% of each run, Pallas kernels for 0% -> 0%
where the time goes in v1:
time: 31.6 us; the launch traced here: 31.3 us
  Pallas kernels  21.9 us (69%)
  local copies, waits for them, and re-layouts  8.67 us (27%)
  between operations  0.66 us (2%)
    pallas_call x1, Pallas kernels, shards(): pl.pallas_call(functools.partial(kernel, ctx_size, head_size, reach, grou...  21.9 us
    unnamed x18, local copies, waits for them, and re-layouts  8.67 us

profile of v1, /device:TPU:0, one launch (start us, length us, event | category | flops | bytes accessed | tf_op | source)
XLA Modules:
  0.0 31.3 jit_solution(11975514325078980198)
XLA Ops:
  0.6 0.0 copy-start.6
  0.6 0.0 copy-start.5
  0.7 0.6 %copy-done.6 = s32[4]{0:T(128)S(1)} copy-done((s32[4]{0:T(128)S(1)}, s32[4]{0:T(128)}, u32[]{:S(2)}) %copy-start.6) | copy-done | bytes 40
  1.3 0.0 copy-done.5
  1.3 0.0 copy-start
  1.3 1.0 %copy-done = bf16[512,512]{1,0:T(8,128)(2,1)S(1)} copy-done((bf16[512,512]{1,0:T(8,128)(2,1)S(1)}, bf16[512,512]{1,0:T(8,128)(2,1)}, u32[]{:S(2)}) %copy-start) | copy-done | bytes 524312
  2.3 0.0 copy-start.1
  2.3 1.0 %copy-done.1 = bf16[512,512]{1,0:T(8,128)(2,1)S(1)} copy-done((bf16[512,512]{1,0:T(8,128)(2,1)S(1)}, bf16[512,512]{1,0:T(8,128)(2,1)}, u32[]{:S(2)}) %copy-start.1) | copy-done | bytes 524312
  3.4 0.0 copy-start.2
  3.4 1.0 %copy-done.2 = bf16[512,512]{1,0:T(8,128)(2,1)S(1)} copy-done((bf16[512,512]{1,0:T(8,128)(2,1)S(1)}, bf16[512,512]{1,0:T(8,128)(2,1)}, u32[]{:S(2)}) %copy-start.2) | copy-done | bytes 524312
  4.4 0.0 copy-start.3
  4.4 1.0 %copy-done.3 = bf16[512,512]{1,0:T(8,128)(2,1)S(1)} copy-done((bf16[512,512]{1,0:T(8,128)(2,1)S(1)}, bf16[512,512]{1,0:T(8,128)(2,1)}, u32[]{:S(2)}) %copy-start.3) | copy-done | bytes 524312
  5.5 0.0 copy-start.4
  5.5 0.7 %copy-done.4 = f32[512]{0:T(512)S(1)} copy-done((f32[512]{0:T(512)S(1)}, f32[512]{0:T(512)}, u32[]{:S(2)}) %copy-start.4) | copy-done | bytes 2072
  6.2 21.9 %shard_map.102 = (bf16[512,512]{1,0:T(8,128)(2,1)S(1)}, bf16[512,512]{1,0:T(8,128)(2,1)S(1)}, bf16[512,512]{1,0:T(8,128)(2,1)S(1)}, bf16[512,512]{1,0:T(8,128)(2,1)S(1)}) custom-call(bf16[512,512]{1,0:T(8,128)(2,1)S(1)} %copy-done, bf16[512,512]{1,0:T(8,128)(2,1)S(1)} %copy-done.1, bf16[512,512]{1,0:T(8,128)(2,1)S(1)} %copy-done.2, ...), custom_call_target="tpu_custom_call" | custom-call | tf_op jit(solution)/shard_map/pallas_call | solution.py:282
  28.1 0.8 %copy.15 = bf16[512,512]{1,0:T(8,128)(2,1)} copy(bf16[512,512]{1,0:T(8,128)(2,1)S(1)} %get-tuple-element.8) | data formatting | bytes 1048576
  28.9 0.8 %copy.16 = bf16[512,512]{1,0:T(8,128)(2,1)} copy(bf16[512,512]{1,0:T(8,128)(2,1)S(1)} %get-tuple-element.9) | data formatting | bytes 1048576
  29.7 0.8 %copy.17 = bf16[512,512]{1,0:T(8,128)(2,1)} copy(bf16[512,512]{1,0:T(8,128)(2,1)S(1)} %get-tuple-element.10) | data formatting | bytes 1048576
  30.5 0.8 %copy.18 = bf16[512,512]{1,0:T(8,128)(2,1)} copy(bf16[512,512]{1,0:T(8,128)(2,1)S(1)} %get-tuple-element.11) | data formatting | bytes 1048576
Async XLA Ops:
  0.6 0.7 %copy-start.6 = (s32[4]{0:T(128)S(1)}, s32[4]{0:T(128)}, u32[]{:S(2)}) copy-start(s32[4]{0:T(128)} %level_ref.1) | copy-start | bytes 52
  0.6 0.7 %copy-start.5 = (s32[16]{0:T(128)S(1)}, s32[16]{0:T(128)}, u32[]{:S(2)}) copy-start(s32[16]{0:T(128)} %len_ref.1) | copy-start | bytes 196
  1.3 1.0 %copy-start = (bf16[512,512]{1,0:T(8,128)(2,1)S(1)}, bf16[512,512]{1,0:T(8,128)(2,1)}, u32[]{:S(2)}) copy-start(bf16[512,512]{1,0:T(8,128)(2,1)} %q_ref.1) | copy-start | bytes 1572868
  2.3 1.0 %copy-start.1 = (bf16[512,512]{1,0:T(8,128)(2,1)S(1)}, bf16[512,512]{1,0:T(8,128)(2,1)}, u32[]{:S(2)}) copy-start(bf16[512,512]{1,0:T(8,128)(2,1)} %k_ref.1) | copy-start | bytes 1572868
  3.4 1.0 %copy-start.2 = (bf16[512,512]{1,0:T(8,128)(2,1)S(1)}, bf16[512,512]{1,0:T(8,128)(2,1)}, u32[]{:S(2)}) copy-start(bf16[512,512]{1,0:T(8,128)(2,1)} %v_ref.1) | copy-start | bytes 1572868
  4.4 1.0 %copy-start.3 = (bf16[512,512]{1,0:T(8,128)(2,1)S(1)}, bf16[512,512]{1,0:T(8,128)(2,1)}, u32[]{:S(2)}) copy-start(bf16[512,512]{1,0:T(8,128)(2,1)} %og_ref.1) | copy-start | bytes 1572868
  5.5 0.7 %copy-start.4 = (f32[512]{0:T(512)S(1)}, f32[512]{0:T(512)}, u32[]{:S(2)}) copy-start(f32[512]{0:T(512)} %param.11) | copy-start | bytes 6148

commit v2 on v1

--- a/solution.py
+++ b/solution.py
@@ -27,12 +27,24 @@
 
 def kernel(
     ctx_size, head_size, reach, group_heads,
-    q_ref, k_ref, v_ref, og_ref, gain_ref, len_ref, level_ref,
+    q_hbm, k_hbm, v_hbm, og_hbm, gain_hbm, len_hbm, level_hbm,
     out_ref, dq_ref, dk_ref, dv_ref,
     far_ref, term_ref, back_ref, stat_ref, stats_ref,
+    q_ref, k_ref, v_ref, og_ref, gain_ref, len_ref, level_ref, load_sem,
     bias_ref, p_ref, pf_ref, ds_ref, sc_ref, o_ref, dqf_ref, own_ref, dkn_ref, dvn_ref,
     far_send, far_recv, back_send, back_recv, stat_send, stat_recv,
 ):
+    loads = [
+        pltpu.make_async_copy(source, target, load_sem.at[i])
+        for i, (source, target) in enumerate(
+            (
+                (k_hbm, k_ref), (v_hbm, v_ref), (len_hbm, len_ref), (level_hbm, level_ref),
+                (q_hbm, q_ref), (gain_hbm, gain_ref), (og_hbm, og_ref),
+            )
+        )
+    ]
+    for load in loads:
+        load.start()
     toks, width = q_ref.shape
     heads = width // HEAD_FEATURES
     picked = toks // DILATION
@@ -51,16 +63,10 @@
     def wide_cols(h):
         return slice(width + h * HEAD_FEATURES, width + (h + 1) * HEAD_FEATURES)
 
+    halves = back_ref.shape[0]
+    part_heads = heads // halves
+
     blocks = [(b * half, (b + 1) * half) for b in range(2)]
-
-    for d in range(1, slots):
-        @pl.when(c < d)
-        def _():
-            far_ref[d] = jnp.zeros(far_ref.shape[1:], BF16)
-
-        @pl.when(c + d >= ctx_size)
-        def _():
-            back_ref[d - 1] = jnp.zeros(back_ref.shape[1:], BF16)
 
     barrier = pltpu.get_barrier_semaphore()
     for d in range(1, slots):
@@ -74,6 +80,18 @@
     for e in range(1, head_size):
         peer = lax.rem(hp + e, head_size)
         pl.semaphore_signal(barrier, inc=1, device_id=(c, peer), device_id_type=MESH)
+
+    for d in range(1, slots):
+        @pl.when(c < d)
+        def _():
+            far_ref[d] = jnp.zeros(far_ref.shape[1:], BF16)
+
+        @pl.when(c + d >= ctx_size)
+        def _():
+            back_ref[:, d - 1] = jnp.zeros((halves,) + back_ref.shape[2:], BF16)
+
+    loads[0].wait()
+    loads[1].wait()
 
     def offset_of(h):
         return lax.rem(hp * heads + h, DILATION)
@@ -96,10 +114,10 @@
             device_id=(c + d, hp), device_id_type=MESH,
         )
 
-    def back_copy(d):
+    def back_copy(part, d):
         return pltpu.make_async_remote_copy(
-            src_ref=term_ref.at[d - 1], dst_ref=back_ref.at[d - 1],
-            send_sem=back_send.at[d - 1], recv_sem=back_recv.at[d - 1],
+            src_ref=term_ref.at[part, d - 1], dst_ref=back_ref.at[part, d - 1],
+            send_sem=back_send.at[part, d - 1], recv_sem=back_recv.at[part, d - 1],
             device_id=(c - d, hp), device_id_type=MESH,
         )
 
@@ -114,6 +132,9 @@
         @pl.when(c + d < ctx_size)
         def _():
             far_copy(d).start()
+
+    for load in loads[2:]:
+        load.wait()
 
     place_q = iota((1, toks), 1) + c * toks
     first = jnp.zeros((1, toks), jnp.int32)
@@ -210,17 +231,18 @@
         value_term = dot(weight, grad, 1, 1)
         own_ref[:, cols(h)] = key_term[0:picked]
         own_ref[:, wide_cols(h)] = value_term[0:picked]
-        term_ref[:, :, cols(h)] = (
+        part, spot = divmod(h, part_heads)
+        term_ref[part, :, :, cols(spot)] = (
             key_term[picked:].astype(BF16).reshape(reach, picked, HEAD_FEATURES)
         )
-        term_ref[:, :, wide_cols(h)] = (
+        term_ref[part, :, :, cols(spot + part_heads)] = (
             value_term[picked:].astype(BF16).reshape(reach, picked, HEAD_FEATURES)
         )
-
-    for d in range(1, slots):
-        @pl.when(c >= d)
-        def _():
-            back_copy(d).start()
+        if spot == part_heads - 1:
+            for d in reversed(range(1, slots)):
+                @pl.when(c >= d)
+                def _():
+                    back_copy(part, d).start()
 
     for h in range(heads):
         grad = (sc_ref[h] * near_scale[h]).astype(BF16)
@@ -239,22 +261,28 @@
             )
             dvn_ref[low:high, cols(h)] = dot(p_ref[h, low:high, low:toks], grad[:, low:toks], 1, 1)
 
-    for d in range(1, slots):
-        @pl.when(c + d < ctx_size)
-        def _():
-            back_copy(d).wait_recv()
-    mine = own_ref[...]
-    for d in range(1, slots):
-        mine = mine + back_ref[d - 1].astype(F32)
-    upper = mine.astype(BF16)
-    lower = (mine - upper.astype(F32)).astype(BF16)
-    both = jnp.concatenate([upper, lower], axis=0)
     spot = iota((toks, 2 * picked), 0)
     target = iota((toks, 2 * picked), 1) % picked * DILATION
-    for h in range(heads):
-        place = jnp.where(spot == target + offset_of(h), 1.0, 0.0).astype(BF16)
-        dk_ref[:, cols(h)] = (dkn_ref[:, cols(h)] + dot(place, both[:, cols(h)])).astype(BF16)
-        dv_ref[:, cols(h)] = (dvn_ref[:, cols(h)] + dot(place, both[:, wide_cols(h)])).astype(BF16)
+    for part in range(halves):
+        for d in range(1, slots):
+            @pl.when(c + d < ctx_size)
+            def _():
+                back_copy(part, d).wait_recv()
+        theirs = back_ref[part, 0].astype(F32)
+        for d in range(2, slots):
+            theirs = theirs + back_ref[part, d - 1].astype(F32)
+        for inner in range(part_heads):
+            h = part * part_heads + inner
+            place = jnp.where(spot == target + offset_of(h), 1.0, 0.0).astype(BF16)
+            for near, out, own, column in (
+                (dkn_ref, dk_ref, cols(h), inner),
+                (dvn_ref, dv_ref, wide_cols(h), inner + part_heads),
+            ):
+                mine = own_ref[:, own] + theirs[:, cols(column)]
+                upper = mine.astype(BF16)
+                lower = (mine - upper.astype(F32)).astype(BF16)
+                both = jnp.concatenate([upper, lower], axis=0)
+                out[:, cols(h)] = (near[:, cols(h)] + dot(place, both)).astype(BF16)
 
     for d in range(1, slots):
         @pl.when(c + d < ctx_size)
@@ -263,9 +291,22 @@
 
         @pl.when(c >= d)
         def _():
-            back_copy(d).wait_send()
+            for part in range(halves):
+                back_copy(part, d).wait_send()
     for e in range(1, head_size):
         stat_copy(e).wait_send()
+
+
+def store(*refs):
+    count = len(refs) // 2
+    sems = refs[-1]
+    copies = [
+        pltpu.make_async_copy(refs[i], refs[count + i], sems.at[i]) for i in range(count)
+    ]
+    for copy in copies:
+        copy.start()
+    for copy in copies:
+        copy.wait()
 
 
 def shards(queries, keys, values, out_grad, norm_gain, doc_lengths, group_level):
@@ -277,19 +318,30 @@
     reach = max(ctx_size // 2, 1)
     slots = reach + 1
     vmem = pl.BlockSpec(memory_space=pltpu.VMEM)
-    smem = pl.BlockSpec(memory_space=pltpu.SMEM)
+    hbm = pl.BlockSpec(memory_space=pltpu.HBM)
+    halves = 2 if heads % 2 == 0 else 1
     grads = jax.ShapeDtypeStruct((toks, width), BF16)
-    return pl.pallas_call(
+    gain = norm_gain.reshape(1, width)
+    operands = (queries, keys, values, out_grad, gain, doc_lengths, group_level)
+    results = pl.pallas_call(
         functools.partial(kernel, ctx_size, head_size, reach, group_heads),
         out_shape=(grads,) * 4,
-        in_specs=[vmem] * 5 + [smem] * 2,
+        in_specs=[hbm] * 7,
         out_specs=(vmem,) * 4,
         scratch_shapes=[
             pltpu.VMEM((slots, picked, 2 * width), BF16),
-            pltpu.VMEM((reach, picked, 2 * width), BF16),
-            pltpu.VMEM((reach, picked, 2 * width), BF16),
+            pltpu.VMEM((halves, reach, picked, 2 * width // halves), BF16),
+            pltpu.VMEM((halves, reach, picked, 2 * width // halves), BF16),
             pltpu.VMEM((8, toks), F32),
             pltpu.VMEM((head_size - 1, 8, toks), F32),
+            pltpu.VMEM((toks, width), BF16),
+            pltpu.VMEM((toks, width), BF16),
+            pltpu.VMEM((toks, width), BF16),
+            pltpu.VMEM((toks, width), BF16),
+            pltpu.VMEM((1, width), F32),
+            pltpu.SMEM(doc_lengths.shape, jnp.int32),
+            pltpu.SMEM(group_level.shape, jnp.int32),
+            pltpu.SemaphoreType.DMA((7,)),
             pltpu.VMEM((toks, toks), F32),
             pltpu.VMEM((heads, toks, toks), BF16),
             pltpu.VMEM((heads, slots * picked, toks), BF16),
@@ -302,15 +354,22 @@
             pltpu.VMEM((toks, width), F32),
             pltpu.SemaphoreType.DMA((reach,)),
             pltpu.SemaphoreType.DMA((reach,)),
-            pltpu.SemaphoreType.DMA((reach,)),
-            pltpu.SemaphoreType.DMA((reach,)),
+            pltpu.SemaphoreType.DMA((halves, reach)),
+            pltpu.SemaphoreType.DMA((halves, reach)),
             pltpu.SemaphoreType.DMA((head_size - 1,)),
             pltpu.SemaphoreType.DMA((head_size - 1,)),
         ],
         compiler_params=pltpu.CompilerParams(
             collective_id=0, has_side_effects=True, vmem_limit_bytes=48 * 1024 * 1024
         ),
-    )(queries, keys, values, out_grad, norm_gain.reshape(1, width), doc_lengths, group_level)
+    )(*(pltpu.with_memory_space_constraint(given, pltpu.HBM) for given in operands))
+    return pl.pallas_call(
+        store,
+        out_shape=(grads,) * 4,
+        in_specs=[vmem] * 4,
+        out_specs=(hbm,) * 4,
+        scratch_shapes=[pltpu.SemaphoreType.DMA((4,))],
+    )(*results)
 
 
 def solution(mesh):

time: 31.6 us -> 27.6 us (0.87)
  local copies, waits for them, and re-layouts: 8.67 us -> 3.18 us
  Pallas kernels: 21.9 us -> 23.6 us
    unnamed x18 -> x8, local copies, waits for them, and re-layouts: 8.67 us -> 3.18 us
    pallas_call x0 -> x1, Pallas kernels: none -> 2.86 us  [shards(): pl.pallas_call(store, out_shape=(grads,) * 4, in_specs=[vmem] * 4, out_sp...]
    pallas_call x1, Pallas kernels: 21.9 us -> 20.8 us  [shards(): pl.pallas_call(functools.partial(kernel, ctx_size, head_size, reach, grou...]
where the time goes in v2:
time: 27.6 us; the launch traced here: 27.5 us
  Pallas kernels  23.6 us (86%)
  local copies, waits for them, and re-layouts  3.18 us (12%)
  between operations  0.65 us (2%)
    pallas_call x1, Pallas kernels, shards(): pl.pallas_call(functools.partial(kernel, ctx_size, head_size, reach, grou...  20.8 us
    unnamed x8, local copies, waits for them, and re-layouts  3.18 us
    pallas_call x1, Pallas kernels, shards(): pl.pallas_call(store, out_shape=(grads,) * 4, in_specs=[vmem] * 4, out_sp...  2.86 us

profile of v2, /device:TPU:0, one launch (start us, length us, event | category | flops | bytes accessed | tf_op | source)
XLA Modules:
  0.0 27.5 jit_solution(17604827319093218065)
XLA Ops:
  0.6 20.8 %shard_map.102 = (bf16[512,512]{1,0:T(8,128)(2,1)S(1)}, bf16[512,512]{1,0:T(8,128)(2,1)S(1)}, bf16[512,512]{1,0:T(8,128)(2,1)S(1)}, bf16[512,512]{1,0:T(8,128)(2,1)S(1)}) custom-call(bf16[512,512]{1,0:T(8,128)(2,1)} %q_hbm.1, bf16[512,512]{1,0:T(8,128)(2,1)} %k_hbm.1, bf16[512,512]{1,0:T(8,128)(2,1)} %v_hbm.1, bf16[512,512]{1,0:T(8,128)(2,1)} %og_hbm.1, ...), custom_call_target="tpu_custom_call" | custom-call | tf_op jit(solution)/shard_map/pallas_call | solution.py:326
  21.4 0.0 copy-start
  21.4 0.8 %copy-done = bf16[512,512]{1,0:T(8,128)(2,1)} copy-done((bf16[512,512]{1,0:T(8,128)(2,1)}, bf16[512,512]{1,0:T(8,128)(2,1)S(1)}, u32[]{:S(2)}) %copy-start) | copy-done | bytes 524312
  22.2 0.0 copy-start.1
  22.2 0.8 %copy-done.1 = bf16[512,512]{1,0:T(8,128)(2,1)} copy-done((bf16[512,512]{1,0:T(8,128)(2,1)}, bf16[512,512]{1,0:T(8,128)(2,1)S(1)}, u32[]{:S(2)}) %copy-start.1) | copy-done | bytes 524312
  23.0 0.0 copy-start.2
  23.0 0.8 %copy-done.2 = bf16[512,512]{1,0:T(8,128)(2,1)} copy-done((bf16[512,512]{1,0:T(8,128)(2,1)}, bf16[512,512]{1,0:T(8,128)(2,1)S(1)}, u32[]{:S(2)}) %copy-start.2) | copy-done | bytes 524312
  23.8 0.0 copy-start.3
  23.8 0.8 %copy-done.3 = bf16[512,512]{1,0:T(8,128)(2,1)} copy-done((bf16[512,512]{1,0:T(8,128)(2,1)}, bf16[512,512]{1,0:T(8,128)(2,1)S(1)}, u32[]{:S(2)}) %copy-start.3) | copy-done | bytes 524312
  24.6 2.9 %shard_map.103 = (bf16[512,512]{1,0:T(8,128)(2,1)}, bf16[512,512]{1,0:T(8,128)(2,1)}, bf16[512,512]{1,0:T(8,128)(2,1)}, bf16[512,512]{1,0:T(8,128)(2,1)}) custom-call(bf16[512,512]{1,0:T(8,128)(2,1)} %copy-done, bf16[512,512]{1,0:T(8,128)(2,1)} %copy-done.1, bf16[512,512]{1,0:T(8,128)(2,1)} %copy-done.2, bf16[512,512]{1,0:T(8,128)(2,1)} %copy-done.3), custom_call_target="tpu_custom_call" | custom-call | tf_op jit(solution)/shard_map/pallas_call | solution.py:366
Async XLA Ops:
  21.4 0.8 %copy-start = (bf16[512,512]{1,0:T(8,128)(2,1)}, bf16[512,512]{1,0:T(8,128)(2,1)S(1)}, u32[]{:S(2)}) copy-start(bf16[512,512]{1,0:T(8,128)(2,1)S(1)} %get-tuple-element.8.refs_0_) | copy-start | bytes 1572868
  22.2 0.8 %copy-start.1 = (bf16[512,512]{1,0:T(8,128)(2,1)}, bf16[512,512]{1,0:T(8,128)(2,1)S(1)}, u32[]{:S(2)}) copy-start(bf16[512,512]{1,0:T(8,128)(2,1)S(1)} %get-tuple-element.9.refs_1_) | copy-start | bytes 1572868
  23.0 0.8 %copy-start.2 = (bf16[512,512]{1,0:T(8,128)(2,1)}, bf16[512,512]{1,0:T(8,128)(2,1)S(1)}, u32[]{:S(2)}) copy-start(bf16[512,512]{1,0:T(8,128)(2,1)S(1)} %get-tuple-element.10.refs_2_) | copy-start | bytes 1572868
  23.8 0.8 %copy-start.3 = (bf16[512,512]{1,0:T(8,128)(2,1)}, bf16[512,512]{1,0:T(8,128)(2,1)S(1)}, u32[]{:S(2)}) copy-start(bf16[512,512]{1,0:T(8,128)(2,1)S(1)} %get-tuple-element.11.refs_3_) | copy-start | bytes 1572868

commit v3 on v2

--- a/solution.py
+++ b/solution.py
@@ -25,13 +25,47 @@
     return lax.broadcasted_iota(jnp.int32, shape, dim)
 
 
+def cols(h):
+    return slice(h * HEAD_FEATURES, (h + 1) * HEAD_FEATURES)
+
+
+def blocks_of(toks):
+    return [(0, toks // 2), (toks // 2, toks)]
+
+
+def near_backward(h, q_ref, k_ref, v_ref, p_ref, ds_ref, sc_ref, o_ref, dqf_ref, near_ref, dq_ref):
+    toks = q_ref.shape[0]
+    blocks = blocks_of(toks)
+    scale = HEAD_FEATURES ** (-0.5)
+    grad = (sc_ref[h] * near_ref[h]).astype(BF16)
+    delta = jnp.sum(grad.astype(F32) * o_ref[h], axis=0, keepdims=True)
+    keys_t = k_ref[:, cols(h)].T
+    for low, high in blocks:
+        product = dot(v_ref[0:high, cols(h)], grad[:, low:high])
+        weight = p_ref[h, 0:high, low:high].astype(F32)
+        slope = (weight * (product - delta[:, low:high])).astype(BF16)
+        ds_ref[0:high, low:high] = slope
+        query_grad = dot(keys_t[:, 0:high], slope) + dqf_ref[h, :, low:high]
+        dq_ref[low:high, cols(h)] = (query_grad * scale).T.astype(BF16)
+    return [
+        (
+            low,
+            high,
+            dot(ds_ref[low:high, low:toks], q_ref[low:toks, cols(h)]) * scale,
+            dot(p_ref[h, low:high, low:toks], grad[:, low:toks], 1, 1),
+        )
+        for low, high in blocks
+    ]
+
+
 def kernel(
     ctx_size, head_size, reach, group_heads,
     q_hbm, k_hbm, v_hbm, og_hbm, gain_hbm, len_hbm, level_hbm,
-    out_ref, dq_ref, dk_ref, dv_ref,
+    out_ref, dq_ref, dkn_ref, dvn_ref, own_ref,
+    q_ref, k_ref, v_ref, p_ref, sc_ref, o_ref, dqf_ref, near_ref,
     far_ref, term_ref, back_ref, stat_ref, stats_ref,
-    q_ref, k_ref, v_ref, og_ref, gain_ref, len_ref, level_ref, load_sem,
-    bias_ref, p_ref, pf_ref, ds_ref, sc_ref, o_ref, dqf_ref, own_ref, dkn_ref, dvn_ref,
+    og_ref, gain_ref, len_ref, level_ref, load_sem,
+    bias_ref, pf_ref, ds_ref,
     far_send, far_recv, back_send, back_recv, stat_send, stat_recv,
 ):
     loads = [
@@ -51,22 +85,20 @@
     slots = reach + 1
     far_rows = slots * picked
     half = toks // 2
+    early = dkn_ref.shape[1] // HEAD_FEATURES
     full = width * head_size
     scale = HEAD_FEATURES ** (-0.5)
     scale2 = scale * math.log2(math.e)
     c = lax.axis_index("ctx")
     hp = lax.axis_index("head")
 
-    def cols(h):
-        return slice(h * HEAD_FEATURES, (h + 1) * HEAD_FEATURES)
-
     def wide_cols(h):
         return slice(width + h * HEAD_FEATURES, width + (h + 1) * HEAD_FEATURES)
 
     halves = back_ref.shape[0]
     part_heads = heads // halves
 
-    blocks = [(b * half, (b + 1) * half) for b in range(2)]
+    blocks = blocks_of(toks)
 
     barrier = pltpu.get_barrier_semaphore()
     for d in range(1, slots):
@@ -190,6 +222,7 @@
         weight = weight.astype(BF16)
         pf_ref[h] = weight
         near_scale.append(shrink * inverse)
+        near_ref[h] = near_scale[h]
         far_scale.append(inverse)
         attended = (o_ref[h] * near_scale[h] + dot(far_v, weight, 0, 0) * inverse).astype(BF16)
         attended = attended.astype(F32)
@@ -244,25 +277,13 @@
                 def _():
                     back_copy(part, d).start()
 
-    for h in range(heads):
-        grad = (sc_ref[h] * near_scale[h]).astype(BF16)
-        delta = jnp.sum(grad.astype(F32) * o_ref[h], axis=0, keepdims=True)
-        keys_t = k_ref[:, cols(h)].T
-        for low, high in blocks:
-            product = dot(v_ref[0:high, cols(h)], grad[:, low:high])
-            weight = p_ref[h, 0:high, low:high].astype(F32)
-            slope = (weight * (product - delta[:, low:high])).astype(BF16)
-            ds_ref[0:high, low:high] = slope
-            query_grad = dot(keys_t[:, 0:high], slope) + dqf_ref[h, :, low:high]
-            dq_ref[low:high, cols(h)] = (query_grad * scale).T.astype(BF16)
-        for low, high in blocks:
-            dkn_ref[low:high, cols(h)] = (
-                dot(ds_ref[low:high, low:toks], q_ref[low:toks, cols(h)]) * scale
-            )
-            dvn_ref[low:high, cols(h)] = dot(p_ref[h, low:high, low:toks], grad[:, low:toks], 1, 1)
-
-    spot = iota((toks, 2 * picked), 0)
-    target = iota((toks, 2 * picked), 1) % picked * DILATION
+    for h in range(early):
+        for low, high, key_part, value_part in near_backward(
+            h, q_ref, k_ref, v_ref, p_ref, ds_ref, sc_ref, o_ref, dqf_ref, near_ref, dq_ref
+        ):
+            dkn_ref[low:high, cols(h)] = key_part
+            dvn_ref[low:high, cols(h)] = value_part
+
     for part in range(halves):
         for d in range(1, slots):
             @pl.when(c + d < ctx_size)
@@ -273,16 +294,10 @@
             theirs = theirs + back_ref[part, d - 1].astype(F32)
         for inner in range(part_heads):
             h = part * part_heads + inner
-            place = jnp.where(spot == target + offset_of(h), 1.0, 0.0).astype(BF16)
-            for near, out, own, column in (
-                (dkn_ref, dk_ref, cols(h), inner),
-                (dvn_ref, dv_ref, wide_cols(h), inner + part_heads),
-            ):
-                mine = own_ref[:, own] + theirs[:, cols(column)]
-                upper = mine.astype(BF16)
-                lower = (mine - upper.astype(F32)).astype(BF16)
-                both = jnp.concatenate([upper, lower], axis=0)
-                out[:, cols(h)] = (near[:, cols(h)] + dot(place, both)).astype(BF16)
+            own_ref[:, cols(h)] = own_ref[:, cols(h)] + theirs[:, cols(inner)]
+            own_ref[:, wide_cols(h)] = (
+                own_ref[:, wide_cols(h)] + theirs[:, cols(inner + part_heads)]
+            )
 
     for d in range(1, slots):
         @pl.when(c + d < ctx_size)
@@ -297,14 +312,55 @@
         stat_copy(e).wait_send()
 
 
-def store(*refs):
-    count = len(refs) // 2
-    sems = refs[-1]
-    copies = [
-        pltpu.make_async_copy(refs[i], refs[count + i], sems.at[i]) for i in range(count)
-    ]
-    for copy in copies:
+def finish(
+    out_ref, dqe_ref, dkn_ref, dvn_ref, own_ref,
+    q_ref, k_ref, v_ref, p_ref, sc_ref, o_ref, dqf_ref, near_ref,
+    out_hbm, dq_hbm, dk_hbm, dv_hbm,
+    dq_ref, dk_ref, dv_ref, ds_ref, out_sem, head_sem,
+):
+    toks, width = q_ref.shape
+    heads = width // HEAD_FEATURES
+    picked = own_ref.shape[0]
+    early = dkn_ref.shape[1] // HEAD_FEATURES
+    copies = [pltpu.make_async_copy(out_ref, out_hbm, out_sem.at[0])]
+    copies[0].start()
+
+    def send(h, i, source, target):
+        copy = pltpu.make_async_copy(
+            source.at[:, cols(h)], target.at[:, cols(h)], head_sem.at[h, i]
+        )
         copy.start()
+        copies.append(copy)
+
+    for h in range(early):
+        send(h, 0, dqe_ref, dq_hbm)
+    spot = iota((toks, 2 * picked), 0)
+    target = iota((toks, 2 * picked), 1) % picked * DILATION
+    for h in range(heads):
+        offset = lax.rem(lax.axis_index("head") * heads + h, DILATION)
+        place = jnp.where(spot == target + offset, 1.0, 0.0).astype(BF16)
+        wholes = []
+        for column in (h, heads + h):
+            mine = own_ref[:, cols(column)]
+            upper = mine.astype(BF16)
+            lower = (mine - upper.astype(F32)).astype(BF16)
+            wholes.append(jnp.concatenate([upper, lower], axis=0))
+        if h < early:
+            parts = [
+                (low, high, dkn_ref[low:high, cols(h)], dvn_ref[low:high, cols(h)])
+                for low, high in blocks_of(toks)
+            ]
+        else:
+            parts = near_backward(
+                h, q_ref, k_ref, v_ref, p_ref, ds_ref, sc_ref, o_ref, dqf_ref, near_ref, dq_ref
+            )
+            send(h, 0, dq_ref, dq_hbm)
+        for low, high, key_part, value_part in parts:
+            rows = place[low:high]
+            dk_ref[low:high, cols(h)] = (key_part + dot(rows, wholes[0])).astype(BF16)
+            dv_ref[low:high, cols(h)] = (value_part + dot(rows, wholes[1])).astype(BF16)
+        send(h, 1, dk_ref, dk_hbm)
+        send(h, 2, dv_ref, dv_hbm)
     for copy in copies:
         copy.wait()
 
@@ -317,17 +373,34 @@
     picked = toks // DILATION
     reach = max(ctx_size // 2, 1)
     slots = reach + 1
+    early = heads // 2
     vmem = pl.BlockSpec(memory_space=pltpu.VMEM)
     hbm = pl.BlockSpec(memory_space=pltpu.HBM)
     halves = 2 if heads % 2 == 0 else 1
     grads = jax.ShapeDtypeStruct((toks, width), BF16)
+    across = (heads, HEAD_FEATURES, toks)
+    held = (
+        pltpu.VMEM((toks, width), BF16),
+        pltpu.VMEM((toks, width), BF16),
+        pltpu.VMEM((toks, early * HEAD_FEATURES), F32),
+        pltpu.VMEM((toks, early * HEAD_FEATURES), F32),
+        pltpu.VMEM((picked, 2 * width), F32),
+        pltpu.VMEM((toks, width), BF16),
+        pltpu.VMEM((toks, width), BF16),
+        pltpu.VMEM((toks, width), BF16),
+        pltpu.VMEM((heads, toks, toks), BF16),
+        pltpu.VMEM(across, F32),
+        pltpu.VMEM(across, F32),
+        pltpu.VMEM(across, F32),
+        pltpu.VMEM((heads, 1, toks), F32),
+    )
     gain = norm_gain.reshape(1, width)
     operands = (queries, keys, values, out_grad, gain, doc_lengths, group_level)
     results = pl.pallas_call(
         functools.partial(kernel, ctx_size, head_size, reach, group_heads),
-        out_shape=(grads,) * 4,
+        out_shape=held,
         in_specs=[hbm] * 7,
-        out_specs=(vmem,) * 4,
+        out_specs=(vmem,) * len(held),
         scratch_shapes=[
             pltpu.VMEM((slots, picked, 2 * width), BF16),
             pltpu.VMEM((halves, reach, picked, 2 * width // halves), BF16),
@@ -335,23 +408,13 @@
             pltpu.VMEM((8, toks), F32),
             pltpu.VMEM((head_size - 1, 8, toks), F32),
             pltpu.VMEM((toks, width), BF16),
-            pltpu.VMEM((toks, width), BF16),
-            pltpu.VMEM((toks, width), BF16),
-            pltpu.VMEM((toks, width), BF16),
             pltpu.VMEM((1, width), F32),
             pltpu.SMEM(doc_lengths.shape, jnp.int32),
             pltpu.SMEM(group_level.shape, jnp.int32),
             pltpu.SemaphoreType.DMA((7,)),
             pltpu.VMEM((toks, toks), F32),
-            pltpu.VMEM((heads, toks, toks), BF16),
             pltpu.VMEM((heads, slots * picked, toks), BF16),
             pltpu.VMEM((toks, toks), BF16),
-            pltpu.VMEM((heads, HEAD_FEATURES, toks), F32),
-            pltpu.VMEM((heads, HEAD_FEATURES, toks), F32),
-            pltpu.VMEM((heads, HEAD_FEATURES, toks), F32),
-            pltpu.VMEM((picked, 2 * width), F32),
-            pltpu.VMEM((toks, width), F32),
-            pltpu.VMEM((toks, width), F32),
             pltpu.SemaphoreType.DMA((reach,)),
             pltpu.SemaphoreType.DMA((reach,)),
             pltpu.SemaphoreType.DMA((halves, reach)),
@@ -360,15 +423,23 @@
             pltpu.SemaphoreType.DMA((head_size - 1,)),
         ],
         compiler_params=pltpu.CompilerParams(
-            collective_id=0, has_side_effects=True, vmem_limit_bytes=48 * 1024 * 1024
+            collective_id=0, has_side_effects=True, vmem_limit_bytes=32 * 1024 * 1024
         ),
     )(*(pltpu.with_memory_space_constraint(given, pltpu.HBM) for given in operands))
     return pl.pallas_call(
-        store,
+        finish,
         out_shape=(grads,) * 4,
-        in_specs=[vmem] * 4,
+        in_specs=[vmem] * len(held),
         out_specs=(hbm,) * 4,
-        scratch_shapes=[pltpu.SemaphoreType.DMA((4,))],
+        scratch_shapes=[
+            pltpu.VMEM((toks, width), BF16),
+            pltpu.VMEM((toks, width), BF16),
+            pltpu.VMEM((toks, width), BF16),
+            pltpu.VMEM((toks, toks), BF16),
+            pltpu.SemaphoreType.DMA((1,)),
+            pltpu.SemaphoreType.DMA((heads, 3)),
+        ],
+        compiler_params=pltpu.CompilerParams(vmem_limit_bytes=24 * 1024 * 1024),
     )(*results)
 
 

time: 27.6 us -> 23.8 us (0.86)
  local copies, waits for them, and re-layouts: 3.18 us -> 0 us
  Pallas kernels: 23.6 us -> 23 us
    unnamed x8 -> x0, local copies, waits for them, and re-layouts: 3.18 us -> none
    pallas_call x1, Pallas kernels: 2.86 us -> 2.48 us  [shards(): pl.pallas_call(finish, out_shape=(grads,) * 4, in_specs=[vmem] * len(held...]
where the time goes in v3:
time: 23.8 us; the launch traced here: 23.7 us
  Pallas kernels  23 us (97%)
  between operations  0.64 us (3%)
    pallas_call x1, Pallas kernels, shards(): pl.pallas_call(functools.partial(kernel, ctx_size, head_size, reach, grou...  20.5 us
    pallas_call x1, Pallas kernels, shards(): pl.pallas_call(finish, out_shape=(grads,) * 4, in_specs=[vmem] * len(held...  2.48 us

profile of v3, /device:TPU:0, one launch (start us, length us, event | category | flops | bytes accessed | tf_op | source)
XLA Modules:
  0.0 23.7 jit_solution(11540487498458160570)
XLA Ops:
  0.6 20.5 %shard_map.102 = (bf16[512,512]{1,0:T(8,128)(2,1)S(1)}, bf16[512,512]{1,0:T(8,128)(2,1)S(1)}, f32[512,256]{1,0:T(8,128)S(1)}, f32[512,256]{1,0:T(8,128)S(1)}, f3...) custom-call(bf16[512,512]{1,0:T(8,128)(2,1)} %q_hbm.1, ...), custom_call_target="tpu_custom_call" | custom-call | tf_op jit(solution)/shard_map/pallas_call | solution.py:399
  21.2 2.5 %shard_map.103 = (bf16[512,512]{1,0:T(8,128)(2,1)}, bf16[512,512]{1,0:T(8,128)(2,1)}, bf16[512,512]{1,0:T(8,128)(2,1)}, bf16[512,512]{1,0:T(8,128)(2,1)}) custom-call(bf16[512,512]{1,0:T(8,128)(2,1)S(1)} %get-tuple-element.17.out_ref, bf16[512,512]{1,0:T(8,128)(2,1)S(1)} %get-tuple-element.18.dqe_ref, f32[512,256]{1,0:T(8,128)S(1)} %get-tuple-element.19.dkn_ref, ...), custom_call_target="tpu_custom_call" | custom-call | tf_op jit(solution)/shard_map/pallas_call | solution.py:429

commit v4 on v3

--- a/solution.py
+++ b/solution.py
@@ -77,7 +77,7 @@
             )
         )
     ]
-    for load in loads:
+    for load in loads[:4]:
         load.start()
     toks, width = q_ref.shape
     heads = width // HEAD_FEATURES
@@ -95,8 +95,10 @@
     def wide_cols(h):
         return slice(width + h * HEAD_FEATURES, width + (h + 1) * HEAD_FEATURES)
 
-    halves = back_ref.shape[0]
-    part_heads = heads // halves
+    parts_back = back_ref.shape[0]
+    part_heads = heads // parts_back
+    far_parts = far_ref.shape[0]
+    far_heads = heads // far_parts
 
     blocks = blocks_of(toks)
 
@@ -116,35 +118,54 @@
     for d in range(1, slots):
         @pl.when(c < d)
         def _():
-            far_ref[d] = jnp.zeros(far_ref.shape[1:], BF16)
+            far_ref[:, d] = jnp.zeros((far_parts,) + far_ref.shape[2:], BF16)
 
         @pl.when(c + d >= ctx_size)
         def _():
-            back_ref[:, d - 1] = jnp.zeros((halves,) + back_ref.shape[2:], BF16)
+            back_ref[:, d - 1] = jnp.zeros((parts_back,) + back_ref.shape[2:], BF16)
 
     loads[0].wait()
     loads[1].wait()
+    for load in loads[4:]:
+        load.start()
 
     def offset_of(h):
         return lax.rem(hp * heads + h, DILATION)
 
     row_of = iota((picked, toks), 0) * DILATION
     place_in = iota((picked, toks), 1)
-    for h in range(heads):
-        pick = jnp.where(place_in == row_of + offset_of(h), 1.0, 0.0).astype(BF16)
-        far_ref[0, :, cols(h)] = dot(pick, k_ref[:, cols(h)]).astype(BF16)
-        far_ref[0, :, wide_cols(h)] = dot(pick, v_ref[:, cols(h)]).astype(BF16)
+    def pick_part(part):
+        for spot in range(far_heads):
+            h = part * far_heads + spot
+            pick = jnp.where(place_in == row_of + offset_of(h), 1.0, 0.0).astype(BF16)
+            far_ref[part, 0, :, cols(spot)] = dot(pick, k_ref[:, cols(h)]).astype(BF16)
+            far_ref[part, 0, :, cols(spot + far_heads)] = dot(pick, v_ref[:, cols(h)]).astype(BF16)
+
+    def far_rows_of(h):
+        part, spot = divmod(h, far_heads)
+        shape = (far_rows, HEAD_FEATURES)
+        return (
+            far_ref[part, :, :, cols(spot)].reshape(shape),
+            far_ref[part, :, :, cols(spot + far_heads)].reshape(shape),
+        )
+
+    def far_copy(part, d):
+        return pltpu.make_async_remote_copy(
+            src_ref=far_ref.at[part, 0], dst_ref=far_ref.at[part, d],
+            send_sem=far_send.at[part, d - 1], recv_sem=far_recv.at[part, d - 1],
+            device_id=(c + d, hp), device_id_type=MESH,
+        )
 
     before = jnp.minimum(c, reach)
     after = jnp.minimum(ctx_size - 1 - c, reach)
-    pl.semaphore_wait(barrier, before + after + (head_size - 1))
-
-    def far_copy(d):
-        return pltpu.make_async_remote_copy(
-            src_ref=far_ref.at[0], dst_ref=far_ref.at[d],
-            send_sem=far_send.at[d - 1], recv_sem=far_recv.at[d - 1],
-            device_id=(c + d, hp), device_id_type=MESH,
-        )
+    for part in range(far_parts):
+        pick_part(part)
+        if part == 0:
+            pl.semaphore_wait(barrier, before + after + (head_size - 1))
+        for d in range(1, slots):
+            @pl.when(c + d < ctx_size)
+            def _():
+                far_copy(part, d).start()
 
     def back_copy(part, d):
         return pltpu.make_async_remote_copy(
@@ -159,11 +180,6 @@
             send_sem=stat_send.at[e - 1], recv_sem=stat_recv.at[e - 1],
             device_id=(c, lax.rem(hp + e, head_size)), device_id_type=MESH,
         )
-
-    for d in range(1, slots):
-        @pl.when(c + d < ctx_size)
-        def _():
-            far_copy(d).start()
 
     for load in loads[2:]:
         load.wait()
@@ -180,6 +196,7 @@
         bias_ref[0:high, low:high] = jnp.where(seen, 0.0, HIDDEN)
 
     tops, sums = [], []
+    scaled_sum = jnp.zeros((1, toks), F32)
     for h in range(heads):
         values_t = v_ref[:, cols(h)].T
         top_parts, sum_parts = [], []
@@ -196,20 +213,21 @@
         tops.append(jnp.concatenate(top_parts, axis=1))
         sums.append(jnp.concatenate(sum_parts, axis=1))
         scaled = og_ref[:, cols(h)].astype(F32) * gain_ref[:, cols(h)]
-        sc_ref[h] = scaled.T
-
-    for d in range(1, slots):
-        @pl.when(c >= d)
-        def _():
-            far_copy(d).wait_recv()
+        scaled = scaled.T
+        sc_ref[h] = scaled
+        scaled_sum = scaled_sum + jnp.sum(scaled, axis=0, keepdims=True)
 
     row = iota((far_rows, toks), 0)
     counter = (c - row // picked) * picked + row % picked
     near_scale, far_scale = [], []
-    stats = [jnp.zeros((1, toks), F32) for _ in range(4)]
+    stats = [jnp.zeros((1, toks), F32) for _ in range(3)]
     for h in range(heads):
-        far_k = far_ref[:, :, cols(h)].reshape(far_rows, HEAD_FEATURES)
-        far_v = far_ref[:, :, wide_cols(h)].reshape(far_rows, HEAD_FEATURES)
+        if h % far_heads == 0:
+            for d in range(1, slots):
+                @pl.when(c >= d)
+                def _():
+                    far_copy(h // far_heads, d).wait_recv()
+        far_k, far_v = far_rows_of(h)
         level = level_ref[(hp * heads + h) // group_heads]
         skip = jnp.left_shift(jnp.int32(1), level) - 1
         place_k = counter * DILATION + offset_of(h)
@@ -228,9 +246,10 @@
         attended = attended.astype(F32)
         o_ref[h] = attended
         scaled = sc_ref[h]
-        terms = (attended, attended * attended, scaled, scaled * attended)
+        terms = (attended, attended * attended, scaled * attended)
         stats = [s + jnp.sum(t, axis=0, keepdims=True) for s, t in zip(stats, terms)]
 
+    stats.append(scaled_sum)
     for i in range(4):
         stat_ref[i : i + 1, :] = stats[i]
     stat_ref[4:8, :] = jnp.zeros((4, toks), F32)
@@ -242,7 +261,7 @@
     for e in range(1, head_size):
         total = total + stats_ref[e - 1]
     total = total / full
-    mean, square, grad_mean, cross = (total[i : i + 1, :] for i in range(4))
+    mean, square, cross, grad_mean = (total[i : i + 1, :] for i in range(4))
     rstd = lax.rsqrt(square - mean * mean + EPS)
     shift = -mean * rstd
     proj = rstd * (cross - mean * grad_mean)
@@ -250,18 +269,16 @@
     for h in range(heads):
         attended = o_ref[h]
         normed = attended * rstd + shift
-        out_ref[:, cols(h)] = (normed.T * gain_ref[:, cols(h)]).astype(BF16)
         grad = rstd * (sc_ref[h] - grad_mean - normed * proj)
         sc_ref[h] = grad
         grad = (grad * far_scale[h]).astype(BF16)
         delta = jnp.sum(grad.astype(F32) * attended, axis=0, keepdims=True)
-        far_k = far_ref[:, :, cols(h)].reshape(far_rows, HEAD_FEATURES)
-        far_v = far_ref[:, :, wide_cols(h)].reshape(far_rows, HEAD_FEATURES)
+        far_v = far_rows_of(h)[1]
         weight = pf_ref[h]
         slope = (weight.astype(F32) * (dot(far_v, grad) - delta)).astype(BF16)
-        dqf_ref[h] = dot(far_k, slope, 0, 0)
         key_term = dot(slope, q_ref[:, cols(h)]) * scale
         value_term = dot(weight, grad, 1, 1)
+        pf_ref[h] = slope
         own_ref[:, cols(h)] = key_term[0:picked]
         own_ref[:, wide_cols(h)] = value_term[0:picked]
         part, spot = divmod(h, part_heads)
@@ -276,6 +293,11 @@
                 @pl.when(c >= d)
                 def _():
                     back_copy(part, d).start()
+
+    for h in range(heads):
+        dqf_ref[h] = dot(far_rows_of(h)[0], pf_ref[h], 0, 0)
+        normed = o_ref[h] * rstd + shift
+        out_ref[:, cols(h)] = (normed.T * gain_ref[:, cols(h)]).astype(BF16)
 
     for h in range(early):
         for low, high, key_part, value_part in near_backward(
@@ -284,7 +306,7 @@
             dkn_ref[low:high, cols(h)] = key_part
             dvn_ref[low:high, cols(h)] = value_part
 
-    for part in range(halves):
+    for part in range(parts_back):
         for d in range(1, slots):
             @pl.when(c + d < ctx_size)
             def _():
@@ -302,11 +324,12 @@
     for d in range(1, slots):
         @pl.when(c + d < ctx_size)
         def _():
-            far_copy(d).wait_send()
+            for part in range(far_parts):
+                far_copy(part, d).wait_send()
 
         @pl.when(c >= d)
         def _():
-            for part in range(halves):
+            for part in range(parts_back):
                 back_copy(part, d).wait_send()
     for e in range(1, head_size):
         stat_copy(e).wait_send()
@@ -373,10 +396,11 @@
     picked = toks // DILATION
     reach = max(ctx_size // 2, 1)
     slots = reach + 1
-    early = heads // 2
+    early = heads - heads // 4
     vmem = pl.BlockSpec(memory_space=pltpu.VMEM)
     hbm = pl.BlockSpec(memory_space=pltpu.HBM)
-    halves = 2 if heads % 2 == 0 else 1
+    far_parts = 2 if heads % 2 == 0 else 1
+    parts_back = heads
     grads = jax.ShapeDtypeStruct((toks, width), BF16)
     across = (heads, HEAD_FEATURES, toks)
     held = (
@@ -402,9 +426,9 @@
         in_specs=[hbm] * 7,
         out_specs=(vmem,) * len(held),
         scratch_shapes=[
-            pltpu.VMEM((slots, picked, 2 * width), BF16),
-            pltpu.VMEM((halves, reach, picked, 2 * width // halves), BF16),
-            pltpu.VMEM((halves, reach, picked, 2 * width // halves), BF16),
+            pltpu.VMEM((far_parts, slots, picked, 2 * width // far_parts), BF16),
+            pltpu.VMEM((parts_back, reach, picked, 2 * width // parts_back), BF16),
+            pltpu.VMEM((parts_back, reach, picked, 2 * width // parts_back), BF16),
             pltpu.VMEM((8, toks), F32),
             pltpu.VMEM((head_size - 1, 8, toks), F32),
             pltpu.VMEM((toks, width), BF16),
@@ -415,10 +439,10 @@
             pltpu.VMEM((toks, toks), F32),
             pltpu.VMEM((heads, slots * picked, toks), BF16),
             pltpu.VMEM((toks, toks), BF16),
-            pltpu.SemaphoreType.DMA((reach,)),
-            pltpu.SemaphoreType.DMA((reach,)),
-            pltpu.SemaphoreType.DMA((halves, reach)),
-            pltpu.SemaphoreType.DMA((halves, reach)),
+            pltpu.SemaphoreType.DMA((far_parts, reach)),
+            pltpu.SemaphoreType.DMA((far_parts, reach)),
+            pltpu.SemaphoreType.DMA((parts_back, reach)),
+            pltpu.SemaphoreType.DMA((parts_back, reach)),
             pltpu.SemaphoreType.DMA((head_size - 1,)),
             pltpu.SemaphoreType.DMA((head_size - 1,)),
         ],

time: 23.8 us -> 24.8 us (1.042)
  Pallas kernels: 23 us -> 24.1 us
    pallas_call x1, Pallas kernels: 20.5 us -> 22.1 us  [shards(): pl.pallas_call(functools.partial(kernel, ctx_size, head_size, reach, grou...]
    pallas_call x1, Pallas kernels: 2.48 us -> 1.97 us  [shards(): pl.pallas_call(finish, out_shape=(grads,) * 4, in_specs=[vmem] * len(held...]
where the time goes in v4:
time: 24.8 us; the launch traced here: 24.7 us
  Pallas kernels  24.1 us (97%)
  between operations  0.64 us (3%)
    pallas_call x1, Pallas kernels, shards(): pl.pallas_call(functools.partial(kernel, ctx_size, head_size, reach, grou...  22.1 us
    pallas_call x1, Pallas kernels, shards(): pl.pallas_call(finish, out_shape=(grads,) * 4, in_specs=[vmem] * len(held...  1.97 us

profile of v4, /device:TPU:0, one launch (start us, length us, event | category | flops | bytes accessed | tf_op | source)
XLA Modules:
  0.0 24.7 jit_solution(5446915305072985898)
XLA Ops:
  0.6 22.1 %shard_map.102 = (bf16[512,512]{1,0:T(8,128)(2,1)S(1)}, bf16[512,512]{1,0:T(8,128)(2,1)S(1)}, f32[512,384]{1,0:T(8,128)S(1)}, f32[512,384]{1,0:T(8,128)S(1)}, f3...) custom-call(bf16[512,512]{1,0:T(8,128)(2,1)} %q_hbm.1, ...), custom_call_target="tpu_custom_call" | custom-call | tf_op jit(solution)/shard_map/pallas_call | solution.py:423
  22.7 2.0 %shard_map.103 = (bf16[512,512]{1,0:T(8,128)(2,1)}, bf16[512,512]{1,0:T(8,128)(2,1)}, bf16[512,512]{1,0:T(8,128)(2,1)}, bf16[512,512]{1,0:T(8,128)(2,1)}) custom-call(bf16[512,512]{1,0:T(8,128)(2,1)S(1)} %get-tuple-element.17.out_ref, bf16[512,512]{1,0:T(8,128)(2,1)S(1)} %get-tuple-element.18.dqe_ref, f32[512,384]{1,0:T(8,128)S(1)} %get-tuple-element.19.dkn_ref, ...), custom_call_target="tpu_custom_call" | custom-call | tf_op jit(solution)/shard_map/pallas_call | solution.py:453

commit v5 on v4

--- a/solution.py
+++ b/solution.py
@@ -399,8 +399,8 @@
     early = heads - heads // 4
     vmem = pl.BlockSpec(memory_space=pltpu.VMEM)
     hbm = pl.BlockSpec(memory_space=pltpu.HBM)
-    far_parts = 2 if heads % 2 == 0 else 1
-    parts_back = heads
+    far_parts = 1
+    parts_back = 2 if heads % 2 == 0 else 1
     grads = jax.ShapeDtypeStruct((toks, width), BF16)
     across = (heads, HEAD_FEATURES, toks)
     held = (

time: 24.8 us -> 23.3 us (0.940)
  Pallas kernels: 24.1 us -> 22.5 us
    pallas_call x1, Pallas kernels: 22.1 us -> 20.5 us  [shards(): pl.pallas_call(functools.partial(kernel, ctx_size, head_size, reach, grou...]
where the time goes in v5:
time: 23.3 us; the launch traced here: 23.1 us
  Pallas kernels  22.5 us (97%)
  between operations  0.64 us (3%)
    pallas_call x1, Pallas kernels, shards(): pl.pallas_call(functools.partial(kernel, ctx_size, head_size, reach, grou...  20.5 us
    pallas_call x1, Pallas kernels, shards(): pl.pallas_call(finish, out_shape=(grads,) * 4, in_specs=[vmem] * len(held...  1.97 us

profile of v5, /device:TPU:0, one launch (start us, length us, event | category | flops | bytes accessed | tf_op | source)
XLA Modules:
  0.0 23.1 jit_solution(5198593283835743865)
XLA Ops:
  0.6 20.5 %shard_map.102 = (bf16[512,512]{1,0:T(8,128)(2,1)S(1)}, bf16[512,512]{1,0:T(8,128)(2,1)S(1)}, f32[512,384]{1,0:T(8,128)S(1)}, f32[512,384]{1,0:T(8,128)S(1)}, f3...) custom-call(bf16[512,512]{1,0:T(8,128)(2,1)} %q_hbm.1, ...), custom_call_target="tpu_custom_call" | custom-call | tf_op jit(solution)/shard_map/pallas_call | solution.py:423
  21.2 2.0 %shard_map.103 = (bf16[512,512]{1,0:T(8,128)(2,1)}, bf16[512,512]{1,0:T(8,128)(2,1)}, bf16[512,512]{1,0:T(8,128)(2,1)}, bf16[512,512]{1,0:T(8,128)(2,1)}) custom-call(bf16[512,512]{1,0:T(8,128)(2,1)S(1)} %get-tuple-element.17.out_ref, bf16[512,512]{1,0:T(8,128)(2,1)S(1)} %get-tuple-element.18.dqe_ref, f32[512,384]{1,0:T(8,128)S(1)} %get-tuple-element.19.dkn_ref, ...), custom_call_target="tpu_custom_call" | custom-call | tf_op jit(solution)/shard_map/pallas_call | solution.py:453

commit v6 on v5

--- a/solution.py
+++ b/solution.py
@@ -400,7 +400,7 @@
     vmem = pl.BlockSpec(memory_space=pltpu.VMEM)
     hbm = pl.BlockSpec(memory_space=pltpu.HBM)
     far_parts = 1
-    parts_back = 2 if heads % 2 == 0 else 1
+    parts_back = 1
     grads = jax.ShapeDtypeStruct((toks, width), BF16)
     across = (heads, HEAD_FEATURES, toks)
     held = (

time: 23.3 us -> 22.5 us (0.966)
  the two profiles are of different devices: /device:TPU:0 before, /device:TPU:12 now
where the time goes in v6:
time: 22.5 us; the launch traced here: 22.4 us
  Pallas kernels  21.7 us (96%)
  between operations  0.64 us (3%)
    pallas_call x1, Pallas kernels, shards(): pl.pallas_call(functools.partial(kernel, ctx_size, head_size, reach, grou...  19.8 us
    pallas_call x1, Pallas kernels, shards(): pl.pallas_call(finish, out_shape=(grads,) * 4, in_specs=[vmem] * len(held...  1.97 us

profile of v6, /device:TPU:12, one launch (start us, length us, event | category | flops | bytes accessed | tf_op | source)
XLA Modules:
  0.0 22.4 jit_solution(11142176595829659397)
XLA Ops:
  0.6 19.8 %shard_map.102 = (bf16[512,512]{1,0:T(8,128)(2,1)S(1)}, bf16[512,512]{1,0:T(8,128)(2,1)S(1)}, f32[512,384]{1,0:T(8,128)S(1)}, f32[512,384]{1,0:T(8,128)S(1)}, f3...) custom-call(bf16[512,512]{1,0:T(8,128)(2,1)} %q_hbm.1, ...), custom_call_target="tpu_custom_call" | custom-call | tf_op jit(solution)/shard_map/pallas_call | solution.py:423
  20.4 2.0 %shard_map.103 = (bf16[512,512]{1,0:T(8,128)(2,1)}, bf16[512,512]{1,0:T(8,128)(2,1)}, bf16[512,512]{1,0:T(8,128)(2,1)}, bf16[512,512]{1,0:T(8,128)(2,1)}) custom-call(bf16[512,512]{1,0:T(8,128)(2,1)S(1)} %get-tuple-element.17.out_ref, bf16[512,512]{1,0:T(8,128)(2,1)S(1)} %get-tuple-element.18.dqe_ref, f32[512,384]{1,0:T(8,128)S(1)} %get-tuple-element.19.dkn_ref, ...), custom_call_target="tpu_custom_call" | custom-call | tf_op jit(solution)/shard_map/pallas_call | solution.py:453
